TPU v7x, 256 devices: a whole 4x4x8 slice. The times are simulated.
256 devices in a mesh: grp: 2 (over x_lo), mp: 128 (over x_hi, y, z, core).
Axes of the slice: x: 4 (x_hi: 2, x_lo: 2; x = x_hi * 2 + x_lo), y: 4, z: 8, core: 2. Of those that a mesh axis runs over, the one named last changes fastest.
Arguments:
- latents: bfloat16 [8, 1024, 64], P(None, ('grp', 'mp')), may hold values from -6 to 6
- noise: bfloat16 [8, 1024, 64], P(None, ('grp', 'mp')), may hold values from -6 to 6
- steps_t: int32 [8], replicated, may hold values from 20 to 979
- w_in: bfloat16 [2, 64, 3072], P('grp'), may hold values from -0.75 to 0.75
- norm_gain: float32 [2, 3072], P('grp'), may hold values from 0.5 to 1.5
- w_qkv: bfloat16 [2, 16, 3072, 384], P('grp', None, 'mp'), may hold values from -0.109375 to 0.109375
- q_gain: float32 [2, 16, 128], P('grp'), may hold values from 0.25 to 1.75
- k_gain: float32 [2, 16, 128], P('grp'), may hold values from 0.25 to 1.75
- w_out: bfloat16 [2, 2048, 64], P('grp'), may hold values from -0.125 to 0.125
Outputs:
- gen_grad: float32 [8, 1024, 64], P(None, ('grp', 'mp'))
- fake_grad: float32 [16, 3072, 384], P(None, ('grp', 'mp'))
All inputs are finite; a program needn't handle non-finite values.
Results may differ from a plain program's by a relative error of at most 0.0075.
Values may be sent and summed in bfloat16 or wider, within the bound.
A program may use at most 128 MiB of HBM per device.

v0:
```python
import math

import jax
import jax.numpy as jnp
from jax import lax
from jax.sharding import PartitionSpec as P


def partner_2(value, axis, bit):
    mask = 2**bit
    pairs = [(source, source ^ mask) for source in range(lax.axis_size(axis))]
    return lax.ppermute(value, axis, pairs)


def as_sent(x):

    def short(part):
        return part.astype(jnp.bfloat16) if part.dtype == jnp.float32 else part

    return jax.tree.map(short, x)


def passed_along(x, axis, by):
    peers = lax.axis_size(axis)
    pairs = [(i, i + by) for i in range(peers) if 0 <= i + by < peers]
    return lax.ppermute(x, axis, pairs)


def time_embed(t_value, width):
    half = width // 2
    index = jnp.arange(half).astype(jnp.float32)
    freqs = jnp.exp(-math.log(10000.0) * index / half)
    phase = t_value * freqs
    return jnp.concatenate([jnp.sin(phase), jnp.cos(phase)])


def embed_tokens(noisy_rows, weight_in, gain, temb_row):
    x_val = jnp.dot(noisy_rows, weight_in, preferred_element_type=jnp.float32) + temb_row
    scaled = x_val * lax.rsqrt(jnp.mean(x_val * x_val, axis=-1, keepdims=True) + 1e-06) * gain
    return scaled.astype(jnp.bfloat16)


def head_forward(qkv, gain_q, gain_k, out_rows):
    width = gain_q.shape[0]
    query = qkv[:, :width]
    keyed = qkv[:, width : 2 * width]
    value = qkv[:, 2 * width :]
    q_norm = (
        query * lax.rsqrt(jnp.mean(query * query, axis=-1, keepdims=True) + 1e-06) * gain_q
    ).astype(jnp.bfloat16)
    k_norm = (
        keyed * lax.rsqrt(jnp.mean(keyed * keyed, axis=-1, keepdims=True) + 1e-06) * gain_k
    ).astype(jnp.bfloat16)
    scores = lax.dot_general(
        q_norm, k_norm, (((1,), (1,)), ((), ())), preferred_element_type=jnp.float32
    ) * (1.0 / math.sqrt(width))
    expo = jnp.exp(scores)
    probs = (expo / jnp.sum(expo, axis=-1, keepdims=True)).astype(jnp.bfloat16)
    attended = jnp.dot(
        probs, value.astype(jnp.bfloat16), preferred_element_type=jnp.float32
    ).astype(jnp.bfloat16)
    return jnp.dot(attended, out_rows, preferred_element_type=jnp.float32)


def on_device(latents, noise, steps_t, w_in, norm_gain, w_qkv, q_gain, k_gain, w_out):
    n_model = lax.axis_size("mp")
    group_id = lax.axis_index("grp")
    model_id = lax.axis_index("mp")
    heads = w_qkv.shape[1]
    samples = n_model // heads
    head = model_id // samples
    sample = model_id % samples
    piece = latents.shape[1]
    channels = latents.shape[2]
    width = w_in.shape[2]
    triple = w_qkv.shape[3]
    head_size = triple // 3
    length = 2 * n_model * piece
    row_piece = width // (2 * n_model)
    lat_both, noise_both = (
        lax.all_gather(latents, "grp", axis=1, tiled=True),
        lax.all_gather(noise, "grp", axis=1, tiled=True),
    )
    t_float = steps_t.astype(jnp.float32)
    angle = 0.5 * math.pi / 1000.0 * t_float
    alpha = jnp.cos(angle)[:, None, None]
    sigma = jnp.sin(angle)[:, None, None]
    noisy_tok = (
        alpha * lat_both.astype(jnp.float32) + sigma * noise_both.astype(jnp.float32)
    ).astype(jnp.bfloat16)
    w_local = w_qkv[0]
    w_send = jnp.broadcast_to(w_local[:, None], (heads, samples) + w_local.shape[1:]).reshape(
        n_model, w_local.shape[1], triple
    )
    every = lax.all_gather(noisy_tok, "mp", axis=1, tiled=True)
    mine_rows = lax.dynamic_index_in_dim(every, sample, 0, keepdims=False)
    got_weight = lax.all_to_all(w_send, "mp", split_axis=0, concat_axis=1, tiled=True)
    seq_rows = (
        mine_rows.reshape(n_model, 2, piece, channels)
        .transpose(1, 0, 2, 3)
        .reshape(length, channels)
    )
    w_head = got_weight[0]
    temb_row = time_embed(lax.dynamic_index_in_dim(t_float, sample, 0, keepdims=False), width)
    xn_rows = embed_tokens(seq_rows, w_in[0], norm_gain[0], temb_row)
    qkv = jnp.dot(xn_rows, w_head, preferred_element_type=jnp.float32)
    gain_q = lax.dynamic_index_in_dim(q_gain[0], head, 0, keepdims=False)
    gain_k = lax.dynamic_index_in_dim(k_gain[0], head, 0, keepdims=False)
    out_rows = lax.dynamic_slice_in_dim(w_out[0], head * head_size, head_size, 0)
    partial_pred, pullback = jax.vjp(lambda qv: head_forward(qv, gain_q, gain_k, out_rows), qkv)
    gathered = lax.all_to_all(
        partial_pred.reshape(2, n_model, piece, channels).astype(jnp.bfloat16),
        "mp",
        split_axis=1,
        concat_axis=1,
        tiled=True,
    ).astype(jnp.float32)
    pred = jnp.sum(gathered.reshape(2, heads, samples, piece, channels), axis=1)
    other_half = lax.dynamic_index_in_dim(pred, 1 - group_id, 0, keepdims=False)
    mine_half = lax.dynamic_index_in_dim(pred, group_id, 0, keepdims=False)
    partner = partner_2(other_half, "grp", 0)
    gen_grad = jnp.where(group_id == 0, partner - mine_half, mine_half - partner)
    target = lat_both.reshape(samples, 2, piece, channels).transpose(1, 0, 2, 3).astype(jnp.float32)
    dpred = (pred - target) / samples
    d_send = jnp.broadcast_to(dpred[:, None], (2, heads, samples, piece, channels)).reshape(
        2, n_model, piece, channels
    )
    d_got = lax.all_to_all(as_sent(d_send), "mp", split_axis=1, concat_axis=1, tiled=True).astype(
        d_send.dtype
    )
    cot_rows = d_got.reshape(length, channels)

    def fake_terms():
        dqkv = pullback(cot_rows)[0].astype(jnp.bfloat16)
        term = lax.dot_general(
            xn_rows, dqkv, (((0,), (0,)), ((), ())), preferred_element_type=jnp.float32
        )
        return term.astype(jnp.bfloat16)

    def real_terms():
        return jnp.zeros((width, triple), jnp.bfloat16)

    grad_local = lax.cond(group_id == 1, fake_terms, real_terms)
    g_send = grad_local.reshape(2, n_model, row_piece, triple)
    got_terms = lax.all_to_all(g_send, "mp", split_axis=1, concat_axis=1, tiled=True)
    summed = jnp.sum(
        got_terms.reshape(2, heads, samples, row_piece, triple), axis=2, dtype=jnp.float32
    )
    arrived = passed_along(summed[0].astype(jnp.bfloat16), "grp", -1).astype(jnp.float32)
    fake_grad = jnp.where(group_id == 0, arrived, summed[1])
    return (gen_grad, fake_grad)


def solution(mesh):
    return jax.shard_map(
        on_device,
        mesh=mesh,
        in_specs=(
            P(None, ("grp", "mp"), None),
            P(None, ("grp", "mp"), None),
            P(),
            P("grp", None, None),
            P("grp", None),
            P("grp", None, "mp", None),
            P("grp", None, None),
            P("grp", None, None),
            P("grp", None, None),
        ),
        out_specs=(P(None, ("grp", "mp"), None), P(None, ("grp", "mp"), None)),
        check_vma=False,
    )
```

profile of v0, /device:TPU:1, one launch (start us, length us, event | category | flops | bytes accessed | tf_op | source)
XLA Modules:
  0.0 333.9 jit_solution(12441546689165535386)
XLA Ops:
  7.2 2.6 broadcast_in_dim.47
  9.8 16.4 %all-to-all-start = ((bf16[128,24,384]{2,1,0:T(8,128)(2,1)}), bf16[128,24,384]{2,1,0:T(8,128)(2,1)S(1)}, u32[]{:S(2)}, u32[]{:S(2)}) async-start(bf16[128,24,384]{2,1,0:T(8,128)(2,1)} %bitcast.19), calls=%async_computation | async-start | bytes 4718592 | tf_op jit(solution)/shard_map/all_to_all | solution.py:97
  26.3 4.0 %all_gather.10 = bf16[8,8,64]{2,0,1:T(8,128)(2,1)S(1)} all-gather(bf16[8,4,64]{2,0,1:T(8,128)(2,1)S(1)} %copy.73), channel_id=1, replica_groups=mesh['grp'=2,'mp'=128] {'grp'}, dimensions={1}, use_global_device_ids=true | all-gather | bytes 12288 | tf_op jit(solution)/shard_map/all_gather | solution.py:82
  30.3 3.7 %all_gather.9 = bf16[8,8,64]{2,0,1:T(8,128)(2,1)S(1)} all-gather(bf16[8,4,64]{2,0,1:T(8,128)(2,1)S(1)} %copy.72), channel_id=1, replica_groups=mesh['grp'=2,'mp'=128] {'grp'}, dimensions={1}, use_global_device_ids=true | all-gather | bytes 12288 | tf_op jit(solution)/shard_map/all_gather | solution.py:81
  34.1 0.7 add_convert_fusion.2
  34.9 0.6 dynamic_slice.28
  35.4 0.7 constant_dynamic-slice_fusion
  36.2 0.7 fusion.24
  36.9 122.5 %all-gather.2.cloned.1.call-done = bf16[8,1024,64]{2,0,1:T(8,128)(2,1)} async-done(((bf16[8,8,64]{2,0,1:T(8,128)(2,1)}), bf16[8,1024,64]{2,0,1:T(8,128)(2,1)}) %all-gather.2.cloned.1.call-update) | async-done | bytes 1048592 | tf_op jit(solution)/shard_map/all_gather | solution.py:95
  159.3 2.1 constant_dynamic-slice_fusion.2
  161.7 6.3 %multiply_reduce_fusion.2 = (f32[1024]{0:T(1024)S(1)}, f32[1024,3072]{1,0:T(8,128)}) fusion(f32[3072]{0:T(1024)S(1)} %pad_maximum_fusion, bf16[1024,64]{1,0:T(8,128)(2,1)S(1)} %bitcast.89, bf16[1,64,3072]{2,1,0:T(8,128)(2,1)S(1)} %copy-done), kind=kOutput, calls=%fused_computation.33 | convolution fusion | flops 412089344 | bytes 13123584 | tf_op jit(solution)/shard_map/dot_general | solution.py:38
  168.0 9.6 %multiply_convert_fusion = bf16[1024,3072]{1,0:T(8,128)(2,1)} fusion(f32[1024,3072]{1,0:T(8,128)} %get-tuple-element.349, f32[3072]{0:T(1024)S(1)} %bitcast.105, f32[1024]{0:T(1024)S(1)} %add_rsqrt_fusion.2, f32[3072]{0:T(1024)S(1)} %pad_maximum_fusion), kind=kLoop, calls=%fused_computation.32 | loop fusion | flops 12582912 | bytes 18903040 | tf_op jit(solution)/shard_map/convert_element_type | solution.py:40
  177.6 4.8 %fusion.33 = f32[1024,384]{0,1:T(8,128)S(1)} fusion(bf16[1024,3072]{1,0:T(8,128)(2,1)} %multiply_convert_fusion, bf16[3072,384]{1,0:T(8,128)(2,1)S(1)} %bitcast.87), kind=kOutput, calls=%fused_computation.80 | convolution fusion | flops 2415919104 | bytes 10223616 | tf_op jit(solution)/shard_map/dot_general | solution.py:106
  182.6 0.6 copy-done.11
  183.2 1.0 fusion.29
  184.2 0.8 fusion.30
  185.0 0.6 divide_convert_fusion
  185.7 0.8 convolution_convert_fusion.6
  186.5 0.5 copy-done.1
  187.0 0.9 convolution_convert_fusion.7
  187.9 0.2 copy.76
  188.1 0.9 reshape.166
  189.0 8.6 %all-to-all-start.1 = ((bf16[128,2,256]{2,1,0:T(2,128)(2,1)}), bf16[128,2,256]{2,1,0:T(2,128)(2,1)S(1)}, u32[]{:S(2)}, u32[]{:S(2)}) async-start(bf16[128,2,256]{2,1,0:T(2,128)(2,1)} %reshape.166), calls=%async_computation.1 | async-start | bytes 262144 | tf_op jit(solution)/shard_map/all_to_all | solution.py:111
  197.6 13.2 %all-to-all-done.1 = bf16[128,2,256]{2,1,0:T(2,128)(2,1)S(1)} async-done(((bf16[128,2,256]{2,1,0:T(2,128)(2,1)}), bf16[128,2,256]{2,1,0:T(2,128)(2,1)S(1)}, u32[]{:S(2)}, u32[]{:S(2)}) %all-to-all-start.1) | async-done | bytes 131104 | tf_op jit(solution)/shard_map/all_to_all | solution.py:111
  210.8 0.2 reshape.167
  211.1 0.6 copy-done.9
  211.7 0.1 broadcast_in_dim.48
  211.8 0.9 reshape.168
  212.7 5.5 %all-to-all-start.2 = ((bf16[128,2,256]{2,1,0:T(2,128)(2,1)}), bf16[128,2,256]{2,1,0:T(2,128)(2,1)S(1)}, u32[]{:S(2)}, u32[]{:S(2)}) async-start(bf16[128,2,256]{2,1,0:T(2,128)(2,1)} %reshape.168), calls=%async_computation.2 | async-start | bytes 262144 | tf_op jit(solution)/shard_map/all_to_all | solution.py:128
  218.2 0.7 dynamic-slice_bitcast_fusion.1
  218.9 1.8 slice.32
  220.7 10.9 %all-to-all-done.2 = bf16[128,2,256]{2,1,0:T(2,128)(2,1)S(1)} async-done(((bf16[128,2,256]{2,1,0:T(2,128)(2,1)}), bf16[128,2,256]{2,1,0:T(2,128)(2,1)S(1)}, u32[]{:S(2)}, u32[]{:S(2)}) %all-to-all-start.2) | async-done | bytes 131104 | tf_op jit(solution)/shard_map/all_to_all | solution.py:128
  231.6 0.2 reshape.169
  231.8 0.6 conditional.1
  231.8 0.3 broadcast.117
  232.3 2.5 copy.85
  234.8 3.5 %reshape.160 = bf16[2,128,12,384]{3,2,1,0:T(8,128)(2,1)S(1)} reshape(bf16[3072,384]{1,0:T(8,128)(2,1)} %copy.85) | data formatting | bytes 4718592 | tf_op jit(solution)/shard_map/reshape | solution.py:144
  238.3 5.1 %copy.86 = bf16[2,128,12,384]{3,0,2,1:T(2,128)(2,1)} copy(bf16[2,128,12,384]{3,2,1,0:T(8,128)(2,1)S(1)} %reshape.160) | data formatting | bytes 4718592 | tf_op jit(solution)/shard_map/reshape | solution.py:144
  243.4 5.7 %all-to-all-start.3 = ((bf16[2,128,12,384]{3,0,2,1:T(2,128)(2,1)}), bf16[2,128,12,384]{3,0,2,1:T(2,128)(2,1)S(1)}, u32[]{:S(2)}, u32[]{:S(2)}) async-start(bf16[2,128,12,384]{3,0,2,1:T(2,128)(2,1)} %copy.86), calls=%async_computation.3 | async-start | bytes 4718592 | tf_op jit(solution)/shard_map/all_to_all | solution.py:145
  249.1 12.1 %collective-permute-start = (f32[8,4,64]{2,0,1:T(8,128)S(1)}, f32[8,4,64]{2,0,1:T(8,128)S(1)}, u32[]{:S(2)}, u32[]{:S(2)}) collective-permute-start(f32[8,4,64]{2,0,1:T(8,128)S(1)} %dynamic-slice_bitcast_fusion), channel_id=1, source_target_pairs={{0,128},{128,0},{1,129},{129,1},{2,130},{130,2},{3,131},{131,3},{4... | collective-permute-start | bytes 24584 | tf_op jit(solution)/shard_map/ppermute | solution.py:12
  261.3 45.8 %all-to-all-done.3 = bf16[2,128,12,384]{3,0,2,1:T(2,128)(2,1)S(1)} async-done(((bf16[2,128,12,384]{3,0,2,1:T(2,128)(2,1)}), bf16[2,128,12,384]{3,0,2,1:T(2,128)(2,1)S(1)}, u32[]{:S(2)}, u32[]{:S(2)}) %all-to-all-start.3) | async-done | bytes 2359328 | tf_op jit(solution)/shard_map/all_to_all | solution.py:145
  307.1 2.0 convert_reduce_fusion
  309.1 0.2 slice.25
  309.3 1.3 collective-permute-start.1
  310.7 0.6 copy.88
  311.3 0.3 slice.26
  311.6 14.6 %collective-permute-done.1 = bf16[16,12,384]{2,1,0:T(8,128)(2,1)S(1)} collective-permute-done((bf16[16,12,384]{2,1,0:T(8,128)(2,1)S(1)}, bf16[16,12,384]{2,1,0:T(8,128)(2,1)S(1)}, u32[]{:S(2)}, u32[]{:S(2)}) %collective-permute-start.1) | collective-permute-done | bytes 147488 | tf_op jit(solution)/shard_map/ppermute | solution.py:26
  326.2 0.8 copy.89
  (52 shorter events, 0.7 us)
Async XLA Ops:
  7.2 154.5 %copy-start = (bf16[1,64,3072]{2,1,0:T(8,128)(2,1)S(1)}, bf16[1,64,3072]{2,1,0:T(8,128)(2,1)}, u32[]{:S(2)}) copy-start(bf16[1,64,3072]{2,1,0:T(8,128)(2,1)} %param.14) | copy-start | bytes 1179652
  7.2 19.1 %copy-start.18 = (bf16[8,4,64]{2,1,0:T(4,128)(2,1)S(1)}, bf16[8,4,64]{2,1,0:T(4,128)(2,1)}, u32[]{:S(2)}) copy-start(bf16[8,4,64]{2,1,0:T(4,128)(2,1)} %param.12) | copy-start | bytes 12292
  7.2 19.1 %copy-start.19 = (bf16[8,4,64]{2,1,0:T(4,128)(2,1)S(1)}, bf16[8,4,64]{2,1,0:T(4,128)(2,1)}, u32[]{:S(2)}) copy-start(bf16[8,4,64]{2,1,0:T(4,128)(2,1)} %param.11) | copy-start | bytes 12292
  7.2 26.9 %copy-start.24 = (s32[8]{0:T(128)S(1)}, s32[8]{0:T(128)}, u32[]{:S(2)}) copy-start(s32[8]{0:T(128)} %param.13) | copy-start | bytes 100
  9.8 167.8 %all-to-all-start = ((bf16[128,24,384]{2,1,0:T(8,128)(2,1)}), bf16[128,24,384]{2,1,0:T(8,128)(2,1)S(1)}, u32[]{:S(2)}, u32[]{:S(2)}) async-start(bf16[128,24,384]{2,1,0:T(8,128)(2,1)} %bitcast.19), calls=%async_computation | async-start | bytes 4718592 | tf_op jit(solution)/shard_map/all_to_all | solution.py:97
  26.2 133.1 %all-gather.2.cloned.1.call-start = ((), (), s32[]{:S(2)}) async-start(), calls=%async_computation.4 | async-start | bytes 2113536 | tf_op jit(solution)/shard_map/all_gather | solution.py:95
  36.2 147.1 %copy-start.20 = (f32[1,1,128]{2,1,0:T(1,128)}, f32[1,1,128]{2,1,0:T(1,128)S(1)}, u32[]{:S(2)}) copy-start(f32[1,1,128]{2,1,0:T(1,128)S(1)} %get-tuple-element.354) | copy-start | bytes 1540
  36.2 147.1 %copy-start.22 = (f32[1,1,128]{2,1,0:T(1,128)}, f32[1,1,128]{2,1,0:T(1,128)S(1)}, u32[]{:S(2)}) copy-start(f32[1,1,128]{2,1,0:T(1,128)S(1)} %get-tuple-element.355) | copy-start | bytes 1540
  161.6 6.3 %copy-start.17 = (f32[1,3072]{1,0:T(1,128)S(1)}, f32[1,3072]{1,0:T(1,128)}, u32[]{:S(2)}) copy-start(f32[1,3072]{1,0:T(1,128)} %param.15) | copy-start | bytes 36868
  182.4 3.2 copy-start.3
  182.5 0.7 copy-start.11
  182.5 0.7 copy-start.13
  184.2 1.5 copy-start.5
  184.2 1.5 copy-start.7
  185.0 2.0 copy-start.1
  185.0 2.0 copy-start.15
  189.0 21.8 %all-to-all-start.1 = ((bf16[128,2,256]{2,1,0:T(2,128)(2,1)}), bf16[128,2,256]{2,1,0:T(2,128)(2,1)S(1)}, u32[]{:S(2)}, u32[]{:S(2)}) async-start(bf16[128,2,256]{2,1,0:T(2,128)(2,1)} %reshape.166), calls=%async_computation.1 | async-start | bytes 262144 | tf_op jit(solution)/shard_map/all_to_all | solution.py:111
  211.1 0.6 copy-start.9
  212.7 18.9 %all-to-all-start.2 = ((bf16[128,2,256]{2,1,0:T(2,128)(2,1)}), bf16[128,2,256]{2,1,0:T(2,128)(2,1)S(1)}, u32[]{:S(2)}, u32[]{:S(2)}) async-start(bf16[128,2,256]{2,1,0:T(2,128)(2,1)} %reshape.168), calls=%async_computation.2 | async-start | bytes 262144 | tf_op jit(solution)/shard_map/all_to_all | solution.py:128
  243.4 5.8 %copy-start.10 = (f32[2,8,4,64]{3,1,2,0:T(8,128)S(1)}, f32[2,8,4,64]{3,1,2,0:T(8,128)}, u32[]{:S(2)}) copy-start(f32[2,8,4,64]{3,1,2,0:T(8,128)} %copy-done.9) | copy-start | bytes 49156
  243.4 63.7 %all-to-all-start.3 = ((bf16[2,128,12,384]{3,0,2,1:T(2,128)(2,1)}), bf16[2,128,12,384]{3,0,2,1:T(2,128)(2,1)S(1)}, u32[]{:S(2)}, u32[]{:S(2)}) async-start(bf16[2,128,12,384]{3,0,2,1:T(2,128)(2,1)} %copy.86), calls=%async_computation.3 | async-start | bytes 4718592 | tf_op jit(solution)/shard_map/all_to_all | solution.py:145
  249.1 61.5 %collective-permute-start = (f32[8,4,64]{2,0,1:T(8,128)S(1)}, f32[8,4,64]{2,0,1:T(8,128)S(1)}, u32[]{:S(2)}, u32[]{:S(2)}) collective-permute-start(f32[8,4,64]{2,0,1:T(8,128)S(1)} %dynamic-slice_bitcast_fusion), channel_id=1, source_target_pairs={{0,128},{128,0},{1,129},{129,1},{2,130},{130,2},{3,131},{131,3},{4... | collective-permute-start | bytes 24584 | tf_op jit(solution)/shard_map/ppermute | solution.py:12
  309.3 16.8 %collective-permute-start.1 = (bf16[16,12,384]{2,1,0:T(8,128)(2,1)S(1)}, bf16[16,12,384]{2,1,0:T(8,128)(2,1)S(1)}, u32[]{:S(2)}, u32[]{:S(2)}) collective-permute-start(bf16[16,12,384]{2,1,0:T(8,128)(2,1)S(1)} %bitcast.97), channel_id=1, source_target_pairs={{128,0},{129,1},{130,2},{131,3},{132,4},{133,5},{134,6},{135,7},{1... | collective-permute-start | bytes 442376 | tf_op jit(solution)/shard_map/ppermute | solution.py:26
Sparse Core Ops, SparseCore 0:
  34.9 124.3 all-gather.1
where the time goes:
time: 336 us; the launch traced here: 334 us
  waiting for transfers between devices  207 us (62%)
  starting transfers between devices  49.7 us (15%)
  local copies, waits for them, and re-layouts  26.2 us (8%)
  other arithmetic  14.9 us (4%)
  between operations  14.5 us (4%)
  matrix products  13.6 us (4%)
  blocking collectives  7.73 us (2%)
    all_gather x1, waiting for transfers between devices, on_device(): every = lax.all_gather(noisy_tok, 'mp', axis=1, tiled=True)  122 us
    all_to_all x1, waiting for transfers between devices, on_device(): lax.all_to_all(g_send, 'mp', split_axis=1, concat_axis=1, tiled=True)  45.8 us
    all_to_all x1, starting transfers between devices, on_device(): lax.all_to_all(w_send, 'mp', split_axis=0, concat_axis=1, tiled=True)  16.4 us
    ppermute x1, waiting for transfers between devices, passed_along(): return lax.ppermute(x, axis, pairs)  14.6 us
    all_to_all x1, waiting for transfers between devices, on_device(): lax.all_to_all(partial_pred.reshape(2, n_model, piece, channels).astype(j...  13.2 us
    ppermute x1, starting transfers between devices, partner_2(): return lax.ppermute(value, axis, pairs)  12.1 us
    all_to_all x1, waiting for transfers between devices, on_device(): lax.all_to_all(as_sent(d_send), 'mp', split_axis=1, concat_axis=1, tiled=...  10.9 us
    convert_element_type x1, other arithmetic, embed_tokens(): return scaled.astype(jnp.bfloat16)  9.64 us
  transfers between devices with their start and end apart: 7, of which 5 were waited for; matrix products, arithmetic and copies ran while one was open for 8% of the time, Pallas kernels for 0%

commit v1 on v0

v1 whole, which is shorter than its diff:
```python
import functools
import math

import jax
import jax.numpy as jnp
from jax import lax
from jax.experimental import pallas as pl
from jax.experimental.pallas import tpu as pltpu
from jax.sharding import PartitionSpec as P

MESH = pl.DeviceIdType.MESH
XH, NY, NZ, NC = 2, 4, 8, 2
HEADS, SAMPLES = XH * NZ, NY * NC
D, HD, CH, LEN = 3072, 128, 64, 1024
TRIPLE = 3 * HD
BF, F32 = jnp.bfloat16, jnp.float32


def place():
    m = lax.axis_index("mp")
    return (
        lax.axis_index("grp"),
        m // (NY * NZ * NC),
        (m // (NZ * NC)) % NY,
        (m // NC) % NZ,
        m % NC,
    )


def device(g, xh, y, z, c):
    return (g, ((xh * NY + y) * NZ + z) * NC + c)


def rows(start, size, step):
    return pl.ds(pl.multiple_of(start, step), size)


def send(src, dst, ssem, rsem, target):
    copy = pltpu.make_async_remote_copy(
        src_ref=src, dst_ref=dst, send_sem=ssem, recv_sem=rsem, device_id=target, device_id_type=MESH
    )
    copy.start()


def take(ref, sem):
    pltpu.make_async_copy(ref, ref, sem).wait()


def greet(barrier, target):
    pl.semaphore_signal(barrier, inc=1, device_id=target, device_id_type=MESH)


Z_ORDER = (0, 1, 7, 2, 6, 3, 5, 4)


def gather_kernel(
    w_ref, nl_ref, W, NL, w0s, w0r, w1s, n1r, n1f,
    n1_s, n1_r, nz_s, nz_r, nx_s, nx_r, w0_s, w0_r, w_s, w1_r, wa_r, wb_r, wr_r, sb_r,
):
    g, xh, y, z, c = place()
    cross = xh != c
    X = xh * 2 + g
    barrier = pltpu.get_barrier_semaphore()
    for dy in range(NY):
        for dc in range(NC):
            if dy or dc:
                greet(barrier, device(g, xh, (y + dy) % NY, z, (c + dc) % NC))
    for dz in range(1, NZ):
        greet(barrier, device(g, xh, y, (z + dz) % NZ, c))
    for dx in range(1, 4):
        X2 = (X + dx) % 4
        greet(barrier, device(X2 % 2, X2 // 2, y, z, c))

    @pl.when(cross)
    def _():
        for dz in range(NZ):
            greet(barrier, device(g, c, y, (z + dz) % NZ, xh))

    pl.semaphore_wait(barrier, 7 + 7 + 3 + jnp.where(cross, NZ, 0))

    me_b = y * NC + c
    for dy in range(NY):
        for dc in range(NC):
            y2, c2 = (y + dy) % NY, (c + dc) % NC
            b2 = y2 * NC + c2
            if dy or dc:
                send(nl_ref.at[b2], n1r.at[me_b], n1_s, n1_r, device(g, xh, y2, z, c2))
            else:
                pltpu.make_async_copy(nl_ref.at[b2], n1r.at[me_b], n1_r).start()

    for j in range(NZ):
        w0s[j, 0:24, :] = w_ref[(1 - c) * NZ + j]
        w0s[j, 24:32, :] = jnp.zeros((8, TRIPLE), BF)
    send(w0s, w0r, w0_s, w0_r, device(g, xh, y, z, 1 - c))

    take(n1r, n1_r)
    for j in range(SAMPLES):
        n1f[j * 4 : j * 4 + 4, :] = n1r[j, 0:4, :].astype(F32)
    own_n = rows((X * NZ + z) * 32, 32, 32)
    NL[own_n, :] = n1f[...].astype(BF)
    for dz in Z_ORDER[1:]:
        send(NL.at[own_n], NL.at[own_n], nz_s, nz_r, device(g, xh, y, (z + dz) % NZ, c))

    take(w0r, w0_r)
    for j in range(NZ):
        mine = w_ref[c * NZ + j].astype(F32)
        theirs = w0r[j, 0:24, :].astype(F32)
        low = jnp.where(c == 0, mine, theirs)
        high = jnp.where(c == 0, theirs, mine)
        w1s[j] = jnp.concatenate([low, high], axis=0).astype(BF)
    for dz in Z_ORDER:
        z2 = (z + dz) % NZ
        src, dst = w1s.at[z2], W.at[rows(((xh * NY + y) * NZ + z) * 48, 48, 48)]
        if dz:
            send(src, dst, w_s, w1_r.at[dz], device(g, c, y, z2, xh))
        else:

            @pl.when(cross)
            def _():
                send(src, dst, w_s, w1_r.at[dz], device(g, c, y, z2, xh))

            @pl.when(jnp.logical_not(cross))
            def _():
                pltpu.make_async_copy(src, dst, w1_r.at[dz]).start()

    take(NL.at[0 : 7 * 32], nz_r)
    own_x = rows(X * 256, 256, 256)
    for dx in range(1, 4):
        X2 = (X + dx) % 4
        send(NL.at[own_x], NL.at[own_x], nx_s, nx_r, device(X2 % 2, X2 // 2, y, z, c))

    up, down = device(g, xh, (y + 1) % NY, z, c), device(g, xh, (y + 3) % NY, z, c)
    sib = device(g, xh, y, z, 1 - c)

    def piece(dy, dz):
        return W.at[rows(((c * NY + (y + dy) % NY) * NZ + (z + 8 - dz) % NZ) * 48, 48, 48)]

    def pass_on(ref, rsem, target):
        send(ref, ref, w_s, rsem, target)

    for s in range(NZ + 4):
        if s < NZ:
            dz = Z_ORDER[s]
            ref = piece(0, dz)
            take(ref, w1_r.at[dz])
            pass_on(ref, wa_r.at[dz], up)
            pass_on(ref, wb_r.at[dz], down)
            pass_on(ref, sb_r, sib)
        if 2 <= s < NZ + 2:
            dz = Z_ORDER[s - 2]
            ref = piece(3, dz)
            take(ref, wa_r.at[dz])
            if s % 2 == 0:
                pass_on(ref, wr_r.at[dz], up)
            pass_on(ref, sb_r, sib)
            ref = piece(1, dz)
            take(ref, wb_r.at[dz])
            if s % 2 == 1:
                pass_on(ref, wr_r.at[dz], down)
            pass_on(ref, sb_r, sib)
        if s >= 4:
            dz = Z_ORDER[s - 4]
            ref = piece(2, dz)
            take(ref, wr_r.at[dz])
            pass_on(ref, sb_r, sib)

    take(W.at[0 : D // 2], sb_r)
    take(NL.at[0 : 3 * 256], nx_r)
    take(n1r.at[0:7], n1_s)
    take(w0s, w0_s)
    take(NL.at[0 : 7 * 32], nz_s)
    take(NL.at[0 : 3 * 256], nx_s)
    take(W.at[0 : 63 * 48], w_s)

    @pl.when(cross)
    def _():
        take(W.at[0:48], w_s)


DMA = pltpu.SemaphoreType.DMA
VM = pl.BlockSpec(memory_space=pltpu.VMEM)


def params(cid):
    return pltpu.CompilerParams(
        collective_id=cid, has_side_effects=True, vmem_limit_bytes=48 * 1024 * 1024
    )


def gather(w_local, nl_send):
    return pl.pallas_call(
        gather_kernel,
        out_shape=(jax.ShapeDtypeStruct((D, TRIPLE), BF), jax.ShapeDtypeStruct((LEN, 128), BF)),
        in_specs=[VM, VM],
        out_specs=(VM, VM),
        scratch_shapes=[
            pltpu.VMEM((NZ, 32, TRIPLE), BF),
            pltpu.VMEM((NZ, 32, TRIPLE), BF),
            pltpu.VMEM((NZ, 48, TRIPLE), BF),
            pltpu.VMEM((SAMPLES, 16, 128), BF),
            pltpu.VMEM((32, 128), F32),
            DMA, DMA, DMA, DMA, DMA, DMA, DMA, DMA, DMA,
            DMA((NZ,)), DMA((NZ,)), DMA((NZ,)), DMA((NZ,)), DMA,
        ],
        compiler_params=params(0),
        name="gather",
    )(w_local, nl_send)


def pred_kernel(
    pp, lat, gen, cot, p1r, dch, pmine, pother, gs, p1_s, p1_r, d_s, d_r, x_s, x_r, g_s, g_r
):
    g, xh, y, z, c = place()
    h, me_b = xh * NZ + z, y * NC + c
    barrier = pltpu.get_barrier_semaphore()
    for dh in range(1, HEADS):
        h2 = (h + dh) % HEADS
        greet(barrier, device(g, h2 // NZ, y, h2 % NZ, c))
    for dy in range(NY):
        for dc in range(NC):
            if dy or dc:
                greet(barrier, device(g, xh, (y + dy) % NY, z, (c + dc) % NC))
    greet(barrier, device(1 - g, xh, y, z, c))
    pl.semaphore_wait(barrier, 15 + 7 + 1)

    for dh in range(1, HEADS):
        h2 = (h + dh) % HEADS
        send(pp.at[rows(h2 * 32, 32, 32)], p1r.at[h], p1_s, p1_r, device(g, h2 // NZ, y, h2 % NZ, c))
    pltpu.make_async_copy(pp.at[rows(h * 32, 32, 32)], p1r.at[h], p1_r).start()
    take(p1r, p1_r)
    pred = jnp.sum(p1r[...].astype(F32), axis=0)
    pmine[...] = pred
    partner = device(1 - g, xh, y, z, c)
    send(pmine, pother, x_s, x_r, partner)

    @pl.when(g == 1)
    def _():
        dch[...] = ((pred - lat[...].astype(F32)) * (1.0 / SAMPLES)).astype(BF)
        own = rows(h * 32, 32, 32)
        for dh in range(1, HEADS):
            h2 = (h + dh) % HEADS
            send(dch, cot.at[own], d_s, d_r, device(g, h2 // NZ, y, h2 % NZ, c))
        pltpu.make_async_copy(dch, cot.at[own], d_r).start()

    take(pother, x_r)
    diff = jnp.where(g == 0, pother[...] - pmine[...], pmine[...] - pother[...])
    low = diff[:, 0:CH]
    high = diff[:, CH:]
    mine = jnp.where(g == 0, low, high)
    for j in range(SAMPLES):
        gs[j, 0:4, 0:CH] = mine[j * 4 : j * 4 + 4, :]
    for dy in range(NY):
        for dc in range(NC):
            y2, c2 = (y + dy) % NY, (c + dc) % NC
            b2 = y2 * NC + c2
            if dy or dc:
                send(gs.at[b2], gen.at[me_b], g_s, g_r, device(g, xh, y2, z, c2))
            else:
                pltpu.make_async_copy(gs.at[b2], gen.at[me_b], g_r).start()
    take(gen, g_r)
    take(pmine, x_s)
    take(gs.at[0:7], g_s)
    take(p1r.at[0:15], p1_s)

    @pl.when(g == 1)
    def _():
        take(cot, d_r)
        take(p1r.at[0:15], d_s)


def reduce_pred(pp, lat):
    return pl.pallas_call(
        pred_kernel,
        out_shape=(
            jax.ShapeDtypeStruct((SAMPLES, 8, 128), F32),
            jax.ShapeDtypeStruct((LEN // 2, 128), BF),
        ),
        in_specs=[VM, VM],
        out_specs=(VM, VM),
        scratch_shapes=[
            pltpu.VMEM((HEADS, 32, 128), BF),
            pltpu.VMEM((32, 128), BF),
            pltpu.VMEM((32, 128), F32),
            pltpu.VMEM((32, 128), F32),
            pltpu.VMEM((SAMPLES, 8, 128), F32),
            DMA, DMA, DMA, DMA, DMA, DMA, DMA, DMA,
        ],
        compiler_params=params(1),
        name="reduce_pred",
    )(pp, lat)


HALF, PART = D // 2, 192


def scatter_kernel(
    term, R, sibr, rel_s, rel_r, st, yst, yr, fin, sb_s, sb_r, rl_s, rl_r, y_s, y_r, f_s, f_r
):
    g, xh, y, z, c = place()
    h = xh * NZ + z
    barrier = pltpu.get_barrier_semaphore()
    fake = g == 1

    def is_me(xh2, z2, c2):
        return (xh2 == xh) & (z2 == z) & (c2 == c) & fake

    def targets():
        for dx in range(XH):
            for dz in Z_ORDER:
                for dc in range(NC):
                    yield (xh + dx) % XH, (z + dz) % NZ, (c + dc) % NC

    for dx in range(XH):
        for dz in range(NZ):
            xh2, z2 = (xh + dx) % XH, (z + dz) % NZ

            @pl.when(jnp.logical_not(is_me(xh2, z2, g)))
            def _():
                greet(barrier, device(1, xh2, y, z2, g))

    @pl.when(fake)
    def _():
        up, down = device(1, xh, (y + 1) % NY, z, c), device(1, xh, (y + 3) % NY, z, c)
        sib = device(1, xh, y, z, 1 - c)
        for t in (up, down, sib):
            greet(barrier, t)
        pl.semaphore_wait(barrier, 3 + 32 - c)

        def part(j, x2):
            return (x2 * NY + (y + j) % NY) * PART

        for j in (2, 1, 3, 0):
            for x2 in range(XH):
                src = term.at[rows((1 - c) * HALF + part(j, x2), PART, 16)]
                send(src, sibr.at[rows(part(j, x2), PART, 16)], sb_s, sb_r.at[j], sib)

        def local(j, x2):
            mine = term[rows(c * HALF + part(j, x2), PART, 16), :].astype(F32)
            return mine + sibr[rows(part(j, x2), PART, 16), :].astype(F32)

        take(sibr.at[0 : 2 * PART], sb_r.at[2])
        for x2, t in ((0, up), (1, down)):
            rel_s[x2] = local(2, x2).astype(BF)
            send(rel_s.at[x2], rel_r.at[x2], rl_s, rl_r.at[x2], t)
        for j, x2, t in ((1, 1, up), (3, 0, down)):
            take(sibr.at[0 : 2 * PART], sb_r.at[j])
            yst[j // 2, x2] = local(j, x2).astype(BF)
            send(yst.at[j // 2, x2], yr.at[j // 2, x2], y_s, y_r, t)
        for j, x2, t in ((1, 0, up), (3, 1, down)):
            take(rel_r.at[x2], rl_r.at[x2])
            yst[j // 2, x2] = (local(j, x2) + rel_r[x2].astype(F32)).astype(BF)
            send(yst.at[j // 2, x2], yr.at[j // 2, x2], y_s, y_r, t)
        take(sibr.at[0 : 2 * PART], sb_r.at[0])
        for x2 in range(XH):
            fin[x2] = local(0, x2)
        take(yr, y_r)
        for x2 in range(XH):
            fin[x2] = fin[x2] + yr[0, x2].astype(F32) + yr[1, x2].astype(F32)
        for x2 in range(XH):
            for z2 in range(NZ):
                for c2 in range(NC):
                    i = z2 * NC + c2
                    st[(x2 * NZ + z2) * NC + c2, 0:12, :] = fin[x2, i * 12 : i * 12 + 12, :].astype(BF)
        for xh2, z2, c2 in targets():
            src = st.at[(xh2 * NZ + z2) * NC + c2]
            me = (xh2 == xh) & (z2 == z) & (c2 == c) & (c == 1)

            @pl.when(me)
            def _():
                pltpu.make_async_copy(src, R.at[h], f_r).start()

            @pl.when(jnp.logical_not(me))
            def _():
                send(src, R.at[h], f_s, f_r, device(c, xh2, y, z2, c2))

        take(sibr, sb_s)
        take(rel_s, rl_s)
        take(yst, y_s)
        take(st.at[0:31], f_s)

        @pl.when(c == 0)
        def _():
            take(st.at[0], f_s)

    take(R, f_r)


def scatter_grad(term):
    return pl.pallas_call(
        scatter_kernel,
        out_shape=jax.ShapeDtypeStruct((HEADS, 16, TRIPLE), BF),
        in_specs=[VM],
        out_specs=VM,
        scratch_shapes=[
            pltpu.VMEM((HALF, TRIPLE), BF),
            pltpu.VMEM((XH, PART, TRIPLE), BF),
            pltpu.VMEM((XH, PART, TRIPLE), BF),
            pltpu.VMEM((32, 16, TRIPLE), BF),
            pltpu.VMEM((2, XH, PART, TRIPLE), BF),
            pltpu.VMEM((2, XH, PART, TRIPLE), BF),
            pltpu.VMEM((XH, PART, TRIPLE), F32),
            DMA, DMA((NY,)), DMA, DMA((XH,)), DMA, DMA, DMA, DMA,
        ],
        compiler_params=params(2),
        name="scatter_grad",
    )(term)


def time_embed(t_value, width):
    half = width // 2
    index = jnp.arange(half).astype(jnp.float32)
    freqs = jnp.exp(-math.log(10000.0) * index / half)
    phase = t_value * freqs
    return jnp.concatenate([jnp.sin(phase), jnp.cos(phase)])


def embed_tokens(noisy_rows, weight_in, gain, temb_row):
    x_val = jnp.dot(noisy_rows, weight_in, preferred_element_type=jnp.float32) + temb_row
    scaled = x_val * lax.rsqrt(jnp.mean(x_val * x_val, axis=-1, keepdims=True) + 1e-06) * gain
    return scaled.astype(jnp.bfloat16)


def head_forward(qkv, gain_q, gain_k, out_rows):
    width = gain_q.shape[0]
    query = qkv[:, :width]
    keyed = qkv[:, width : 2 * width]
    value = qkv[:, 2 * width :]
    q_norm = (
        query * lax.rsqrt(jnp.mean(query * query, axis=-1, keepdims=True) + 1e-06) * gain_q
    ).astype(jnp.bfloat16)
    k_norm = (
        keyed * lax.rsqrt(jnp.mean(keyed * keyed, axis=-1, keepdims=True) + 1e-06) * gain_k
    ).astype(jnp.bfloat16)
    scores = lax.dot_general(
        q_norm, k_norm, (((1,), (1,)), ((), ())), preferred_element_type=jnp.float32
    ) * (1.0 / math.sqrt(width))
    expo = jnp.exp(scores)
    probs = (expo / jnp.sum(expo, axis=-1, keepdims=True)).astype(jnp.bfloat16)
    attended = jnp.dot(
        probs, value.astype(jnp.bfloat16), preferred_element_type=jnp.float32
    ).astype(jnp.bfloat16)
    return jnp.dot(attended, out_rows, preferred_element_type=jnp.float32)


def on_device(latents, noise, steps_t, w_in, norm_gain, w_qkv, q_gain, k_gain, w_out):
    g, xh, y, z, c = place()
    head, sample = xh * NZ + z, y * NC + c
    t_float = steps_t.astype(F32)
    angle = 0.5 * math.pi / 1000.0 * t_float
    alpha = jnp.cos(angle)[:, None, None]
    sigma = jnp.sin(angle)[:, None, None]
    noisy = (alpha * latents.astype(F32) + sigma * noise.astype(F32)).astype(BF)
    nl_send = jnp.pad(jnp.concatenate([noisy, latents], axis=-1), ((0, 0), (0, 12), (0, 0)))
    w_head, nl = gather(w_qkv[0], nl_send)
    temb_row = time_embed(lax.dynamic_index_in_dim(t_float, sample, 0, keepdims=False), D)
    xn_rows = embed_tokens(nl[:, :CH], w_in[0], norm_gain[0], temb_row)
    qkv = jnp.dot(xn_rows, w_head, preferred_element_type=F32)
    gain_q = lax.dynamic_index_in_dim(q_gain[0], head, 0, keepdims=False)
    gain_k = lax.dynamic_index_in_dim(k_gain[0], head, 0, keepdims=False)
    out_rows = lax.dynamic_slice_in_dim(w_out[0], head * HD, HD, 0)
    partial_pred, pullback = jax.vjp(lambda qv: head_forward(qv, gain_q, gain_k, out_rows), qkv)
    pp = partial_pred.astype(BF).reshape(XH, 2, 256, CH).transpose(0, 2, 1, 3).reshape(512, 128)
    lat = nl[:, CH:].reshape(XH, 2, 256, CH).transpose(0, 2, 1, 3).reshape(512, 128)
    lat = lax.dynamic_slice_in_dim(lat, head * 32, 32, 0)
    gen, cot = reduce_pred(pp, lat)
    gen_grad = gen[:, :4, :CH]

    def fake_terms():
        cot_rows = cot.reshape(XH, 256, 2, CH).transpose(0, 2, 1, 3).reshape(LEN, CH).astype(F32)
        dqkv = pullback(cot_rows)[0].astype(BF)
        term = lax.dot_general(xn_rows, dqkv, (((0,), (0,)), ((), ())), preferred_element_type=F32)
        return term.astype(BF)

    def real_terms():
        return jnp.zeros((D, TRIPLE), BF)

    term = lax.cond(g == 1, fake_terms, real_terms)
    fake_grad = scatter_grad(term)[:, :12, :].astype(F32)
    return gen_grad, fake_grad


def solution(mesh):
    return jax.shard_map(
        on_device,
        mesh=mesh,
        in_specs=(
            P(None, ("grp", "mp"), None),
            P(None, ("grp", "mp"), None),
            P(),
            P("grp", None, None),
            P("grp", None),
            P("grp", None, "mp", None),
            P("grp", None, None),
            P("grp", None, None),
            P("grp", None, None),
        ),
        out_specs=(P(None, ("grp", "mp"), None), P(None, ("grp", "mp"), None)),
        check_vma=False,
    )
```

time: 336 us -> 143 us (0.43)
  waiting for transfers between devices: 207 us -> 0 us
  Pallas kernels: 0 us -> 98.6 us
  starting transfers between devices: 49.7 us -> 0 us
  between operations: 14.5 us -> 0.96 us
  local copies, waits for them, and re-layouts: 26.2 us -> 13.5 us
  blocking collectives: 7.73 us -> 0 us
    all_gather x1 -> x0, waiting for transfers between devices: 122 us -> none  [on_device(): every = lax.all_gather(noisy_tok, 'mp', axis=1, tiled=True)]
    pallas_call x0 -> x3, Pallas kernels: none -> 98.6 us  [the longest x1 43.7 us: scatter_grad(): pl.pallas_call(scatter_kernel, out_shape=jax.ShapeDtypeStruct((HEADS, 16,...]
    all_to_all x4 -> x0, waiting for transfers between devices: 69.8 us -> none  [the longest x1 45.8 us: on_device(): lax.all_to_all(g_send, 'mp', split_axis=1, concat_axis=1, tiled=True)]
    all_to_all x4 -> x0, starting transfers between devices: 36.2 us -> none  [the longest x1 16.4 us: on_device(): lax.all_to_all(w_send, 'mp', split_axis=0, concat_axis=1, tiled=True)]
    ppermute x2 -> x0, waiting for transfers between devices: 14.6 us -> none  [the longest x1 14.6 us: passed_along(): return lax.ppermute(x, axis, pairs)]
    ppermute x2 -> x0, starting transfers between devices: 13.4 us -> none  [the longest x1 12.1 us: partner_2(): return lax.ppermute(value, axis, pairs)]
    reshape x2 -> x4, local copies, waits for them, and re-layouts: 8.52 us -> 0.45 us  [the longest x3 0.3 us: on_device(): partial_pred.astype(BF).reshape(XH, 2, 256, CH).transpose(0, 2, 1, 3)]
    all_gather x2 -> x0, blocking collectives: 7.73 us -> none  [the longest x1 4 us: on_device(): lax.all_gather(noise, 'grp', axis=1, tiled=True)]
  transfers between devices with their start and end apart: 7 -> 0, of which waited for: 5 -> 0; matrix products, arithmetic and copies ran while one was open for 8% -> 0% of each run, Pallas kernels for 0% -> 0%
where the time goes in v1:
time: 143 us; the launch traced here: 142 us
  Pallas kernels  98.6 us (69%)
  other arithmetic  15 us (10%)
  matrix products  13.9 us (10%)
  local copies, waits for them, and re-layouts  13.5 us (9%)
    pallas_call x1, Pallas kernels, scatter_grad(): pl.pallas_call(scatter_kernel, out_shape=jax.ShapeDtypeStruct((HEADS, 16,...  43.7 us
    pallas_call x1, Pallas kernels, gather(): pl.pallas_call(gather_kernel, out_shape=(jax.ShapeDtypeStruct((D, TRIPLE)...  36.1 us
    pallas_call x1, Pallas kernels, reduce_pred(): pl.pallas_call(pred_kernel, out_shape=(jax.ShapeDtypeStruct((SAMPLES, 8,...  18.8 us
    convert_element_type x1, other arithmetic, embed_tokens(): return scaled.astype(jnp.bfloat16)  9.64 us
    dot_general x1, matrix products, embed_tokens(): jnp.dot(noisy_rows, weight_in, preferred_element_type=jnp.float32)  6.31 us
    dot_general x1, matrix products, on_device(): qkv = jnp.dot(xn_rows, w_head, preferred_element_type=F32)  4.83 us
    unnamed x24, local copies, waits for them, and re-layouts  3.86 us
    cond x1, local copies, waits for them, and re-layouts, on_device(): term = lax.cond(g == 1, fake_terms, real_terms)  3 us

profile of v1, /device:TPU:1, one launch (start us, length us, event | category | flops | bytes accessed | tf_op | source)
XLA Modules:
  0.0 141.9 jit_solution(9917717356259616306)
XLA Ops:
  0.6 0.0 copy-start
  0.7 0.7 convert_element_type.126
  1.4 0.6 dynamic_slice.19
  2.0 0.7 constant_dynamic-slice_fusion.2
  2.7 0.7 multiply_cosine_fusion
  3.4 0.8 add_convert_fusion.2
  4.2 0.7 constant_dynamic-slice_fusion.1
  5.0 0.7 fusion.25
  5.7 0.8 fusion.23.nl_ref
  6.5 0.7 copy.21
  7.2 1.0 copy-done.1
  8.1 36.1 %gather.1 = (bf16[3072,384]{1,0:T(8,128)(2,1)S(1)}, bf16[1024,128]{1,0:T(8,128)(2,1)S(1)}) custom-call(bf16[16,24,384]{2,1,0:T(8,128)(2,1)S(1)} %bitcast.62, bf16[8,16,128]{2,1,0:T(8,128)(2,1)S(1)} %fusion.23.nl_ref), custom_call_target="tpu_custom_call" | custom-call | tf_op jit(solution)/shard_map/gather/pallas_call | solution.py:191
  44.2 0.0 copy-done.8
  44.2 0.1 slice.26
  44.4 0.2 copy.23
  44.6 0.1 constant_dynamic-slice_fusion
  44.7 0.1 copy.37.lat
  44.7 0.0 copy-done
  44.7 0.0 copy-start.12
  44.8 6.3 %multiply_reduce_fusion.2 = (f32[1024]{0:T(1024)S(1)}, f32[1024,3072]{1,0:T(8,128)}) fusion(f32[3072]{0:T(1024)S(1)} %pad_maximum_fusion, bf16[1,64,3072]{2,1,0:T(8,128)(2,1)S(1)} %copy-done, bf16[1024,128]{1,0:T(8,128)(2,1)S(1)} %get-tuple-element.235), kind=kOutput, calls=%fused_computation.33 | convolution fusion | flops 412089344 | bytes 13254656 | tf_op jit(solution)/shard_map/dot_general | solution.py:418
  51.1 0.0 copy-done.12
  51.1 9.6 %multiply_convert_fusion = bf16[1024,3072]{1,0:T(8,128)(2,1)} fusion(f32[1024,3072]{1,0:T(8,128)} %get-tuple-element.294, f32[3072]{0:T(1024)S(1)} %bitcast.78, f32[1024]{0:T(1024)S(1)} %add_rsqrt_fusion.2, f32[3072]{0:T(1024)S(1)} %pad_maximum_fusion), kind=kLoop, calls=%fused_computation.32 | loop fusion | flops 12582912 | bytes 18903040 | tf_op jit(solution)/shard_map/convert_element_type | solution.py:420
  60.7 4.8 %fusion.33 = f32[1024,384]{0,1:T(8,128)S(1)} fusion(bf16[1024,3072]{1,0:T(8,128)(2,1)} %multiply_convert_fusion, bf16[3072,384]{1,0:T(8,128)(2,1)S(1)} %get-tuple-element.236), kind=kOutput, calls=%fused_computation.72 | convolution fusion | flops 2415919104 | bytes 10223616 | tf_op jit(solution)/shard_map/dot_general | solution.py:457
  65.6 0.0 copy-start.4
  65.6 0.1 multiply_reduce_fusion.3
  65.7 0.9 slice.40
  66.6 0.0 copy-done.13
  66.6 0.0 copy-done.15
  66.6 1.0 fusion.29
  67.6 0.8 fusion.30
  68.4 0.0 copy-done.4
  68.4 0.0 copy-start.2
  68.4 0.0 copy-start.9
  68.4 0.0 copy-done.6
  68.4 1.9 %copy-done.2 = f32[1024,1024]{0,1:T(8,128)} copy-done((f32[1024,1024]{0,1:T(8,128)}, f32[1024,1024]{0,1:T(8,128)S(1)}, u32[]{:S(2)}) %copy-start.2) | copy-done | bytes 4194328
  70.3 0.0 copy-done.9
  70.3 0.6 divide_convert_fusion
  71.0 2.0 %fusion.17 = bf16[1024,64]{0,1:T(8,128)(2,1)S(1)} fusion(bf16[1024,1024]{0,1:T(8,128)(2,1)S(1)} %divide_convert_fusion, bf16[1,128,64]{1,2,0:T(8,128)(2,1)} %copy-done.8, f32[1024,384]{0,1:T(8,128)} %copy-done.4), kind=kOutput, calls=%fused_computation.38 | convolution fusion | flops 285409280 | bytes 2506752 | tf_op jit(solution)/shard_map/jvp()/dot_general | solution.py:442
  72.9 0.1 reshape.137
  73.0 0.1 copy.22
  73.2 0.1 copy.25.pp
  73.3 18.8 %reduce_pred.1 = (f32[8,8,128]{2,1,0:T(8,128)S(1)}, bf16[512,128]{1,0:T(8,128)(2,1)}) custom-call(bf16[512,128]{1,0:T(8,128)(2,1)S(1)} %copy.25.pp, bf16[32,128]{1,0:T(8,128)(2,1)S(1)} %copy.37.lat), custom_call_target="tpu_custom_call" | custom-call | tf_op jit(solution)/shard_map/reduce_pred/pallas_call | solution.py:272
  92.1 0.6 slice.27
  92.7 1.7 %conditional.1 = (bf16[3072,384]{0,1:T(8,128)(2,1)}) conditional(s32[]{:T(128)} %convert_element_type.137, () %tuple.28, (bf16[512,128]{1,0:T(8,128)(2,1)}, bf16[128,64]{1,0:T(8,128)(2,1)}, bf16[1024,1024]{0,1:T(8,128)(2,1)S(1)}, bf16[1024,128]{0,1:T(8,128)(2,1)}, f32[1024]{0:T(1024)}, /*index=5*/f32[1024,1024]{0,1:T(8,128)}, ...), branch_computations={%region_4.5_spmd, %region_5.9_spmd} | conditional | flops 3527553024 | bytes 78157048 | solution.py:477
  92.7 1.7 %broadcast.118 = bf16[3072,384]{0,1:T(8,128)(2,1)} broadcast(bf16[]{:T(256)} %constant.123.clone), dimensions={} | broadcast | bytes 2359298 | tf_op jit(solution)/shard_map/broadcast.6
  94.4 3.0 %copy.31.term = bf16[3072,384]{1,0:T(8,128)(2,1)S(1)} copy(bf16[3072,384]{0,1:T(8,128)(2,1)} %get-tuple-element.301) | data formatting | bytes 4718592 | tf_op jit(solution)/shard_map/cond | solution.py:477
  97.4 43.7 %scatter_grad.1 = bf16[16,16,384]{2,1,0:T(8,128)(2,1)S(1)} custom-call(bf16[3072,384]{1,0:T(8,128)(2,1)S(1)} %copy.31.term), custom_call_target="tpu_custom_call" | custom-call | tf_op jit(solution)/shard_map/scatter_grad/pallas_call | solution.py:389
  141.1 0.8 copy.32
  (12 shorter events, 0.1 us)
Async XLA Ops:
  0.6 44.1 %copy-start = (bf16[1,64,3072]{2,1,0:T(8,128)(2,1)S(1)}, bf16[1,64,3072]{2,1,0:T(8,128)(2,1)}, u32[]{:S(2)}) copy-start(bf16[1,64,3072]{2,1,0:T(8,128)(2,1)} %param.14) | copy-start | bytes 1179652
  2.7 63.9 %copy-start.13 = (f32[1,1,128]{2,1,0:T(1,128)}, f32[1,1,128]{2,1,0:T(1,128)S(1)}, u32[]{:S(2)}) copy-start(f32[1,1,128]{2,1,0:T(1,128)S(1)} %get-tuple-element.299) | copy-start | bytes 1540
  2.7 63.9 %copy-start.15 = (f32[1,1,128]{2,1,0:T(1,128)}, f32[1,1,128]{2,1,0:T(1,128)S(1)}, u32[]{:S(2)}) copy-start(f32[1,1,128]{2,1,0:T(1,128)S(1)} %get-tuple-element.300) | copy-start | bytes 1540
  5.0 39.3 %copy-start.8 = (bf16[1,128,64]{1,2,0:T(8,128)(2,1)}, bf16[1,128,64]{1,2,0:T(8,128)(2,1)S(1)}, u32[]{:S(2)}) copy-start(bf16[1,128,64]{1,2,0:T(8,128)(2,1)S(1)} %constant_dynamic-slice_fusion.1) | copy-start | bytes 49156
  7.2 1.0 copy-start.1
  44.7 6.3 %copy-start.12 = (f32[1,3072]{1,0:T(1,128)S(1)}, f32[1,3072]{1,0:T(1,128)}, u32[]{:S(2)}) copy-start(f32[1,3072]{1,0:T(1,128)} %param.15) | copy-start | bytes 36868
  65.6 2.8 %copy-start.4 = (f32[1024,384]{0,1:T(8,128)}, f32[1024,384]{0,1:T(8,128)S(1)}, u32[]{:S(2)}) copy-start(f32[1024,384]{0,1:T(8,128)S(1)} %fusion.33) | copy-start | bytes 4718596
  67.6 0.8 copy-start.6
  68.4 2.0 %copy-start.2 = (f32[1024,1024]{0,1:T(8,128)}, f32[1024,1024]{0,1:T(8,128)S(1)}, u32[]{:S(2)}) copy-start(f32[1024,1024]{0,1:T(8,128)S(1)} %get-tuple-element.296) | copy-start | bytes 12582916
  68.4 2.0 %copy-start.9 = (f32[1024]{0:T(1024)}, f32[1024]{0:T(1024)S(1)}, u32[]{:S(2)}) copy-start(f32[1024]{0:T(1024)S(1)} %get-tuple-element.295) | copy-start | bytes 12292

commit v2 on v0

v2 whole, which is shorter than its diff:
```python
import functools
import math

import jax
import jax.numpy as jnp
from jax import lax
from jax.experimental import pallas as pl
from jax.experimental.pallas import tpu as pltpu
from jax.sharding import PartitionSpec as P

MESH = pl.DeviceIdType.MESH
XH, NY, NZ, NC = 2, 4, 8, 2
HEADS, SAMPLES = XH * NZ, NY * NC
D, HD, CH, LEN = 3072, 128, 64, 1024
TRIPLE = 3 * HD
BF, F32 = jnp.bfloat16, jnp.float32


def place():
    m = lax.axis_index("mp")
    return (
        lax.axis_index("grp"),
        m // (NY * NZ * NC),
        (m // (NZ * NC)) % NY,
        (m // NC) % NZ,
        m % NC,
    )


def device(g, xh, y, z, c):
    return (g, ((xh * NY + y) * NZ + z) * NC + c)


def mod(a, n):
    return lax.rem(a, n)


def rows(start, size, step):
    return pl.ds(pl.multiple_of(start, step), size)


def send(src, dst, ssem, rsem, target):
    copy = pltpu.make_async_remote_copy(
        src_ref=src, dst_ref=dst, send_sem=ssem, recv_sem=rsem, device_id=target, device_id_type=MESH
    )
    copy.start()


def take(ref, sem):
    pltpu.make_async_copy(ref, ref, sem).wait()


def greet(barrier, target):
    pl.semaphore_signal(barrier, inc=1, device_id=target, device_id_type=MESH)


Z_ORDER = (0, 1, 7, 2, 6, 3, 5, 4)


DMA = pltpu.SemaphoreType.DMA
VM = pl.BlockSpec(memory_space=pltpu.VMEM)
SM = pl.BlockSpec(memory_space=pltpu.SMEM)
HALF, PART, QUART = D // 2, 192, 96
TILE = 256
SCALE = 1.0 / math.sqrt(HD)


def dot(a, b, ca=1, cb=0):
    return lax.dot_general(a, b, (((ca,), (cb,)), ((), ())), preferred_element_type=F32)


SCRATCH = dict(
    W=((D, TRIPLE), BF),
    NL=((LEN, 128), BF),
    w0s=((NZ, 32, TRIPLE), BF),
    w0r=((NZ, 32, TRIPLE), BF),
    w1s=((NZ, 48, TRIPLE), BF),
    nst=((SAMPLES, 16, 128), BF),
    n1r=((SAMPLES, 16, 128), BF),
    nsf=((SAMPLES, 16, 128), F32),
    n1f=((32, 128), F32),
    temb=((8, D), F32),
    xf=((128, D), F32),
    xn=((LEN, D), BF),
    xnT=((D, LEN), BF),
    qkv=((LEN, TRIPLE), F32),
    qn=((LEN, HD), BF),
    kn=((LEN, HD), BF),
    v=((LEN, HD), BF),
    knT=((HD, LEN), BF),
    vT=((HD, LEN), BF),
    p32=((4, LEN, TILE), F32),
    pb=((4, LEN, TILE), BF),
    pp=((LEN // 2, 128), BF),
    p1r=((HEADS, 32, 128), BF),
    dch=((32, 128), BF),
    cot=((LEN // 2, 128), BF),
    pmine=((32, 128), F32),
    pother=((32, 128), F32),
    gs=((SAMPLES, 8, 128), F32),
    dq=((LEN, HD), F32),
    dk=((LEN, HD), F32),
    dv=((LEN, HD), F32),
    dqkv=((LEN, TRIPLE), BF),
    T=((D, TRIPLE), BF),
    sibr=((HALF, TRIPLE), BF),
    rel_s=((XH, 2, QUART, TRIPLE), BF),
    rel_r=((XH, 2, QUART, TRIPLE), BF),
    yst=((2, XH, PART, TRIPLE), BF),
    yr=((2, XH, PART, TRIPLE), BF),
    fin=((XH, PART, TRIPLE), F32),
    st=((32, 16, TRIPLE), BF),
)
SEMS = dict(
    n1_s=None, n1_r=None, nz_s=None, nz_r=None, nx_s=None, nx_r=None, w0_s=None, w0_r=None, w_s=None,
    w1_r=NZ, wa_r=NZ, wb_r=NZ, wr_r=NZ, sb_r=None, p1_s=None, p1_r=None, d_s=None, d_r=None,
    x_s=None, x_r=None, g_s=None, g_r=None, ts_s=None, ts_r=NY, rl_s=None, rl_r=(XH, 2), y_s=None,
    y_r=XH, f_s=None, f_r=None,
)
INPUTS = ("lat", "noise", "steps", "w_in", "gain", "w_qkv", "q_gain", "k_gain", "w_out")


class Refs:
    pass


def mega_kernel(*args):
    r = Refs()
    names = INPUTS + ("gen", "R") + tuple(SCRATCH) + tuple(SEMS)
    for name, ref in zip(names, args, strict=True):
        setattr(r, name, ref)
    g, xh, y, z, c = place()
    h, me_b, X = xh * NZ + z, y * NC + c, xh * 2 + g
    fake, cross = g == 1, xh != c
    W, NL = r.W, r.NL

    def yc(dy, dc):
        return mod(y + dy, NY), mod(c + dc, NC)

    def zline(dz):
        return device(g, xh, y, mod(z + dz, NZ), c)

    def xline(dx):
        X2 = mod(X + dx, 4)
        return device(mod(X2, 2), X2 // 2, y, z, c)

    barrier = pltpu.get_barrier_semaphore()
    for dy in range(NY):
        for dc in range(NC):
            if dy or dc:
                y2, c2 = yc(dy, dc)
                greet(barrier, device(g, xh, y2, z, c2))
    for dz in range(1, NZ):
        greet(barrier, zline(dz))
    for dx in range(1, 4):
        greet(barrier, xline(dx))

    @pl.when(cross)
    def _():
        for dz in range(NZ):
            greet(barrier, device(g, c, y, mod(z + dz, NZ), xh))

    for j in range(NZ):
        r.w0s[j, 0:24, :] = r.w_qkv[0, (1 - c) * NZ + j]
        r.w0s[j, 24:32, :] = jnp.zeros((8, TRIPLE), BF)

    rows8 = lax.broadcasted_iota(jnp.int32, (SAMPLES, 128), 0)
    ang = jnp.zeros((SAMPLES, 128), F32)
    for b in range(SAMPLES):
        ang = jnp.where(rows8 == b, r.steps[b].astype(F32), ang)
    ang = 0.5 * math.pi / 1000.0 * ang
    alpha, sigma = jnp.cos(ang), jnp.sin(ang)
    r.nsf[...] = jnp.zeros_like(r.nsf)
    for b in range(SAMPLES):
        latent = r.lat[b].astype(F32)
        noisy = alpha[b : b + 1, 0:CH] * latent + sigma[b : b + 1, 0:CH] * r.noise[b].astype(F32)
        r.nsf[b, 0:4, 0:CH] = noisy
        r.nsf[b, 0:4, CH:128] = latent
    r.nst[...] = r.nsf[...].astype(BF)

    pl.semaphore_wait(barrier, 7 + 7 + 3 + jnp.where(cross, NZ, 0))

    sib = device(g, xh, y, z, 1 - c)
    send(r.w0s, r.w0r, r.w0_s, r.w0_r, sib)
    for dy in range(NY):
        for dc in range(NC):
            y2, c2 = yc(dy, dc)
            src = r.nst.at[y2 * NC + c2]
            if dy or dc:
                send(src, r.n1r.at[me_b], r.n1_s, r.n1_r, device(g, xh, y2, z, c2))
            else:
                pltpu.make_async_copy(src, r.n1r.at[me_b], r.n1_r).start()

    take(r.w0r, r.w0_r)
    for j in range(NZ):
        mine = r.w_qkv[0, c * NZ + j].astype(F32)
        theirs = r.w0r[j, 0:24, :].astype(F32)
        low = jnp.where(c == 0, mine, theirs)
        high = jnp.where(c == 0, theirs, mine)
        r.w1s[j] = jnp.concatenate([low, high], axis=0).astype(BF)
    for dz in Z_ORDER:
        z2 = mod(z + dz, NZ)
        src, dst = r.w1s.at[z2], W.at[rows(((xh * NY + y) * NZ + z) * 48, 48, 48)]
        if dz:
            send(src, dst, r.w_s, r.w1_r.at[dz], device(g, c, y, z2, xh))
        else:

            @pl.when(cross)
            def _():
                send(src, dst, r.w_s, r.w1_r.at[dz], device(g, c, y, z2, xh))

            @pl.when(jnp.logical_not(cross))
            def _():
                pltpu.make_async_copy(src, dst, r.w1_r.at[dz]).start()

    take(r.n1r, r.n1_r)
    for j in range(SAMPLES):
        r.n1f[j * 4 : j * 4 + 4, :] = r.n1r[j, 0:4, :].astype(F32)
    own_n = rows((X * NZ + z) * 32, 32, 32)
    NL[own_n, :] = r.n1f[...].astype(BF)
    for dz in Z_ORDER[1:]:
        send(NL.at[own_n], NL.at[own_n], r.nz_s, r.nz_r, zline(dz))

    up, down = device(g, xh, mod(y + 1, NY), z, c), device(g, xh, mod(y + 3, NY), z, c)

    def piece(dy, dz):
        return W.at[rows(((c * NY + mod(y + dy, NY)) * NZ + mod(z + 8 - dz, NZ)) * 48, 48, 48)]

    def pass_on(ref, rsem, target):
        send(ref, ref, r.w_s, rsem, target)

    def relay(s):
        if s < NZ:
            dz = Z_ORDER[s]
            ref = piece(0, dz)
            take(ref, r.w1_r.at[dz])
            pass_on(ref, r.wa_r.at[dz], up)
            pass_on(ref, r.wb_r.at[dz], down)
            pass_on(ref, r.sb_r, sib)
        if 2 <= s < NZ + 2:
            dz = Z_ORDER[s - 2]
            ref = piece(3, dz)
            take(ref, r.wa_r.at[dz])
            if s % 2 == 0:
                pass_on(ref, r.wr_r.at[dz], up)
            pass_on(ref, r.sb_r, sib)
            ref = piece(1, dz)
            take(ref, r.wb_r.at[dz])
            if s % 2 == 1:
                pass_on(ref, r.wr_r.at[dz], down)
            pass_on(ref, r.sb_r, sib)
        if s >= 4:
            dz = Z_ORDER[s - 4]
            ref = piece(2, dz)
            take(ref, r.wr_r.at[dz])
            pass_on(ref, r.sb_r, sib)

    t_value = r.steps[me_b].astype(F32)
    index = lax.broadcasted_iota(jnp.int32, (1, D // 2), 1).astype(F32)
    phase = t_value * jnp.exp(-math.log(10000.0) * index / (D // 2))
    r.temb[0:1, 0 : D // 2] = jnp.sin(phase)
    r.temb[0:1, D // 2 :] = jnp.cos(phase)

    relay(0)
    relay(1)
    take(NL.at[0 : 7 * 32], r.nz_r)
    own_x = rows(X * 256, 256, 256)
    for dx in range(1, 4):
        send(NL.at[own_x], NL.at[own_x], r.nx_s, r.nx_r, xline(dx))
    relay(2)
    relay(3)

    def embed(tile):
        at = rows(tile * 128, 128, 128)
        noisy = NL[at, :][:, 0:CH]
        total = jnp.zeros((128, 128), F32)
        for k in range(D // 512):
            part = dot(noisy, r.w_in[0, :, k * 512 : k * 512 + 512]) + r.temb[0:1, k * 512 : k * 512 + 512]
            r.xf[:, k * 512 : k * 512 + 512] = part
            sq = part * part
            for i in range(4):
                total = total + sq[:, i * 128 : i * 128 + 128]
        inv = lax.rsqrt(jnp.sum(total, axis=1, keepdims=True) * (1.0 / D) + 1e-06)
        for k in range(D // 512):
            cols = slice(k * 512, k * 512 + 512)
            done = (r.xf[:, cols] * inv * r.gain[0:1, cols]).astype(BF)
            r.xn[at, cols] = done

            @pl.when(fake)
            def _():
                r.xnT[cols, at] = done.T

    embed(X * 2)
    relay(4)
    embed(X * 2 + 1)
    relay(5)
    take(NL.at[0 : 3 * 256], r.nx_r)
    for i in range(6):
        tile = mod(X * 2 + 2 + i, 8)
        embed(tile)
        relay(6 + i)

    def project(half, first):
        cols = rows(half * HALF, HALF, HALF)
        for i in range(4):
            at = slice(i * TILE, i * TILE + TILE)
            part = dot(r.xn[at, cols], W[cols, :])
            r.qkv[at, :] = part if first else r.qkv[at, :] + part

    project(c, True)
    take(W.at[0:HALF], r.sb_r)
    project(1 - c, False)

    gain_q, gain_k = r.q_gain[0, pl.ds(h, 1), :], r.k_gain[0, pl.ds(h, 1), :]

    def normed(lanes):
        raw = r.qkv[:, lanes]
        inv = lax.rsqrt(jnp.mean(raw * raw, axis=-1, keepdims=True) + 1e-06)
        return raw, inv

    q_l, k_l, v_l = slice(0, HD), slice(HD, 2 * HD), slice(2 * HD, TRIPLE)
    raw, inv = normed(q_l)
    r.qn[...] = (raw * inv * gain_q).astype(BF)
    raw, inv = normed(k_l)
    k_norm = (raw * inv * gain_k).astype(BF)
    r.kn[...] = k_norm
    r.knT[...] = k_norm.T
    value = r.qkv[:, v_l].astype(BF)
    r.v[...] = value
    r.vT[...] = value.T
    w_out = r.w_out[0, rows(h * HD, HD, HD), :]

    halves = []
    for t in range(4):
        at = slice(t * TILE, t * TILE + TILE)
        scores = dot(r.kn[...], r.qn[at, :], 1, 1)
        expo = jnp.exp2(scores * (SCALE * math.log2(math.e)))
        probs = expo * (1.0 / jnp.sum(expo, axis=0, keepdims=True))
        r.p32[t] = probs
        probs = probs.astype(BF)
        r.pb[t] = probs
        attended = dot(r.vT[...], probs).astype(BF)
        halves.append(dot(attended.T, w_out))
        if t % 2 == 1:
            x2 = t // 2
            r.pp[x2 * 256 : x2 * 256 + 256, :] = jnp.concatenate(halves, axis=1).astype(BF)
            halves = []
            for dz in Z_ORDER:
                z2 = mod(z + dz, NZ)
                src, dst = r.pp.at[rows((x2 * NZ + z2) * 32, 32, 32)], r.p1r.at[h]
                if dz:
                    send(src, dst, r.p1_s, r.p1_r, device(g, x2, y, z2, c))
                else:

                    @pl.when(xh == x2)
                    def _():
                        pltpu.make_async_copy(src, dst, r.p1_r).start()

                    @pl.when(xh != x2)
                    def _():
                        send(src, dst, r.p1_s, r.p1_r, device(g, x2, y, z2, c))

    take(r.p1r, r.p1_r)
    pred = jnp.sum(r.p1r[...].astype(F32), axis=0)
    r.pmine[...] = pred

    @pl.when(fake)
    def _():
        lat0 = NL[rows((xh * 2 * NZ + z) * 32, 32, 32), :].astype(F32)[:, CH:]
        lat1 = NL[rows(((xh * 2 + 1) * NZ + z) * 32, 32, 32), :].astype(F32)[:, CH:]
        latent = jnp.concatenate([lat0, lat1], axis=1)
        r.dch[...] = ((pred - latent) * (1.0 / SAMPLES)).astype(BF)
        own = rows(h * 32, 32, 32)
        for dx in range(XH):
            for dz in Z_ORDER:
                if dx or dz:
                    target = device(g, mod(xh + dx, XH), y, mod(z + dz, NZ), c)
                    send(r.dch, r.cot.at[own], r.d_s, r.d_r, target)
        pltpu.make_async_copy(r.dch, r.cot.at[own], r.d_r).start()

    partner = device(1 - g, xh, y, z, c)
    send(r.pmine, r.pother, r.x_s, r.x_r, partner)

    def generator():
        take(r.pother, r.x_r)
        diff = jnp.where(g == 0, r.pother[...] - r.pmine[...], r.pmine[...] - r.pother[...])
        mine = jnp.where(g == 0, diff[:, 0:CH], diff[:, CH:])
        for j in range(SAMPLES):
            r.gs[j, 0:4, 0:CH] = mine[j * 4 : j * 4 + 4, :]
        for dy in range(NY):
            for dc in range(NC):
                y2, c2 = yc(dy, dc)
                src, dst = r.gs.at[y2 * NC + c2], r.gen.at[me_b]
                if dy or dc:
                    send(src, dst, r.g_s, r.g_r, device(g, xh, y2, z, c2))
                else:
                    pltpu.make_async_copy(src, dst, r.g_r).start()

    @pl.when(jnp.logical_not(fake))
    def _():
        generator()

    @pl.when(fake)
    def _():
        take(r.cot, r.d_r)
        for t in range(4):
            at = slice(t * TILE, t * TILE + TILE)
            cot = r.cot[(t // 2) * 256 : (t // 2) * 256 + 256, (t % 2) * CH : (t % 2) * CH + CH]
            d_att = dot(cot, w_out, 1, 1).astype(BF)
            d_probs = dot(r.v[...], d_att, 1, 1)
            probs = r.p32[t]
            mean = jnp.sum(probs * d_probs, axis=0, keepdims=True)
            d_score = (probs * (d_probs - mean)).astype(BF)
            dv = dot(r.pb[t], d_att)
            dk = dot(d_score, r.qn[at, :])
            if t:
                r.dv[...] += dv
                r.dk[...] += dk
            else:
                r.dv[...] = dv
                r.dk[...] = dk
            r.dq[at, :] = dot(r.knT[...], d_score).T

        def unnorm(lanes, gain, grad):
            raw, inv = normed(lanes)
            scaled = grad * SCALE * gain
            unit = raw * inv
            inner = jnp.mean(unit * scaled, axis=-1, keepdims=True)
            return (inv * (scaled - unit * inner)).astype(BF)

        r.dqkv[:, q_l] = unnorm(q_l, gain_q, r.dq[...])
        r.dqkv[:, k_l] = unnorm(k_l, gain_k, r.dk[...])
        r.dqkv[:, v_l] = r.dv[...].astype(BF)

        def part(half, j, x2):
            return half * HALF + (x2 * NY + mod(y + j, NY)) * PART

        def block(half, j):
            at0, at1 = rows(part(half, j, 0), PART, PART), rows(part(half, j, 1), PART, PART)
            left = jnp.concatenate([r.xnT[at0, :], r.xnT[at1, :]], axis=0)
            out = dot(left, r.dqkv[...]).astype(BF)
            r.T[at0, :] = out[:PART]
            r.T[at1, :] = out[PART:]

        def to_sibling(j):
            block(1 - c, j)
            for x2 in range(XH):
                src = r.T.at[rows(part(1 - c, j, x2), PART, PART)]
                send(src, r.sibr.at[rows(part(0, j, x2), PART, PART)], r.ts_s, r.ts_r.at[j], sib)

        def arrived(j):
            take(r.sibr.at[0 : 2 * PART], r.ts_r.at[j])

        def local(j, x2, zh=None):
            if zh is None:
                off, size = 0, PART
            else:
                off, size = zh * QUART, QUART
            mine = r.T[rows(part(c, j, x2) + off, size, QUART), :].astype(F32)
            return mine + r.sibr[rows(part(0, j, x2) + off, size, QUART), :].astype(F32)

        def relay_out(x2):
            for zh, t in ((0, up), (1, down)):
                r.rel_s[x2, zh] = local(2, x2, zh).astype(BF)
                send(r.rel_s.at[x2, zh], r.rel_r.at[x2, zh], r.rl_s, r.rl_r.at[x2, zh], t)

        def plain_out(x2):
            for d, j, zh, t in ((0, 1, 1, up), (1, 3, 0, down)):
                at = slice(zh * QUART, zh * QUART + QUART)
                r.yst[d, x2, at, :] = local(j, x2, zh).astype(BF)
                send(r.yst.at[d, x2, at], r.yr.at[d, x2, at], r.y_s, r.y_r.at[x2], t)

        def joined_out(x2):
            for d, j, zh, t in ((0, 1, 0, up), (1, 3, 1, down)):
                at = slice(zh * QUART, zh * QUART + QUART)
                take(r.rel_r.at[x2, zh], r.rl_r.at[x2, zh])
                both = local(j, x2, zh) + r.rel_r[x2, zh].astype(F32)
                r.yst[d, x2, at, :] = both.astype(BF)
                send(r.yst.at[d, x2, at], r.yr.at[d, x2, at], r.y_s, r.y_r.at[x2], t)

        to_sibling(2)
        block(c, 2)
        to_sibling(1)
        to_sibling(3)
        arrived(2)
        relay_out(0)
        block(c, 1)
        block(c, 3)
        arrived(1)
        arrived(3)
        plain_out(0)
        relay_out(1)
        to_sibling(0)
        joined_out(0)
        plain_out(1)
        block(c, 0)
        joined_out(1)
        generator()
        arrived(0)
        for x2 in range(XH):
            take(r.yr.at[:, x2], r.y_r.at[x2])
            r.fin[x2] = local(0, x2) + r.yr[0, x2].astype(F32) + r.yr[1, x2].astype(F32)
            for i in range(NZ * NC):
                r.st[x2 * NZ * NC + i, 0:12, :] = r.fin[x2, i * 12 : i * 12 + 12, :].astype(BF)
            for dz in Z_ORDER:
                for c2 in range(NC):
                    z2 = mod(z + dz, NZ)
                    src = r.st.at[(x2 * NZ + z2) * NC + c2]
                    target = device(c, x2, y, z2, c2)
                    if dz or c2 == 0:
                        send(src, r.R.at[h], r.f_s, r.f_r, target)
                    else:
                        me = (xh == x2) & (c == 1)

                        @pl.when(me)
                        def _():
                            pltpu.make_async_copy(src, r.R.at[h], r.f_r).start()

                        @pl.when(jnp.logical_not(me))
                        def _():
                            send(src, r.R.at[h], r.f_s, r.f_r, target)

        take(r.cot.at[0 : 15 * 32], r.d_s)
        take(r.sibr, r.ts_s)
        take(r.rel_s, r.rl_s)
        take(r.yst, r.y_s)
        take(r.st.at[0:31], r.f_s)

        @pl.when(c == 0)
        def _():
            take(r.st.at[0], r.f_s)

    take(r.n1r.at[0:7], r.n1_s)
    take(r.w0s, r.w0_s)
    take(NL.at[0 : 7 * 32], r.nz_s)
    take(NL.at[0 : 3 * 256], r.nx_s)
    take(W.at[0 : 63 * 48], r.w_s)

    @pl.when(cross)
    def _():
        take(W.at[0:48], r.w_s)

    take(r.p1r.at[0:15], r.p1_s)
    take(r.pmine, r.x_s)
    take(r.gen.at[0:7], r.g_s)
    take(r.gen, r.g_r)
    take(r.R, r.f_r)


def on_device(latents, noise, steps_t, w_in, norm_gain, w_qkv, q_gain, k_gain, w_out):
    gen, grads = pl.pallas_call(
        mega_kernel,
        out_shape=(
            jax.ShapeDtypeStruct((SAMPLES, 8, 128), F32),
            jax.ShapeDtypeStruct((HEADS, 16, TRIPLE), BF),
        ),
        in_specs=[VM, VM, SM, VM, VM, VM, VM, VM, VM],
        out_specs=(VM, VM),
        scratch_shapes=[pltpu.VMEM(*spec) for spec in SCRATCH.values()]
        + [DMA if n is None else DMA(n if isinstance(n, tuple) else (n,)) for n in SEMS.values()],
        compiler_params=pltpu.CompilerParams(
            collective_id=0, has_side_effects=True, vmem_limit_bytes=56 * 1024 * 1024
        ),
        name="distill_step",
    )(latents, noise, steps_t, w_in, norm_gain, w_qkv, q_gain, k_gain, w_out)
    return gen[:, :4, :CH], grads[:, :12, :].astype(F32)


def solution(mesh):
    return jax.shard_map(
        on_device,
        mesh=mesh,
        in_specs=(
            P(None, ("grp", "mp"), None),
            P(None, ("grp", "mp"), None),
            P(),
            P("grp", None, None),
            P("grp", None),
            P("grp", None, "mp", None),
            P("grp", None, None),
            P("grp", None, None),
            P("grp", None, None),
        ),
        out_specs=(P(None, ("grp", "mp"), None), P(None, ("grp", "mp"), None)),
        check_vma=False,
    )
```

time: 336 us -> 93.2 us (0.28)
  the two profiles are of different devices: /device:TPU:1 before, /device:TPU:7 now
where the time goes in v2:
time: 93.2 us; the launch traced here: 93 us
  Pallas kernels  87.3 us (94%)
  local copies, waits for them, and re-layouts  4.12 us (4%)
  other arithmetic  0.95 us (1%)
    pallas_call x1, Pallas kernels, on_device(): pl.pallas_call(mega_kernel, out_shape=(jax.ShapeDtypeStruct((SAMPLES, 8,...  87.3 us
    unnamed x2, local copies, waits for them, and re-layouts  2.75 us

profile of v2, /device:TPU:7, one launch (start us, length us, event | category | flops | bytes accessed | tf_op | source)
XLA Modules:
  0.0 93.0 jit_solution(2794385074133650227)
XLA Ops:
  0.6 1.9 %copy.11.args_8_ = bf16[1,2048,64]{2,1,0:T(8,128)(2,1)} copy(bf16[1,2048,64]{1,2,0:T(8,128)(2,1)} %param.17) | data formatting | bytes 524288 | tf_op args[8]
  2.6 87.3 %distill_step.1 = (f32[8,8,128]{2,1,0:T(8,128)}, bf16[16,16,384]{2,1,0:T(8,128)(2,1)}) custom-call(bf16[8,4,64]{2,1,0:T(4,128)(2,1)} %args_0_.4, bf16[8,4,64]{2,1,0:T(4,128)(2,1)} %args_1_.4, s32[8]{0:T(128)} %args_2_.4, bf16[1,64,3072]{2,1,0:T(8,128)(2,1)} %args_3_.4, f32[1,3072]{1,0:T(1,128)} %args_4_.4, bf16[1,16,24,384]{3,2,1,0:T(8,128)(2,1)} %args_5_.4, ...), custom_call_target="tpu_custom_call" | custom-call | tf_op jit(solution)/shard_map/distill_step/pallas_call | solution.py:551
  89.9 1.4 %slice.6 = f32[8,4,64]{2,1,0:T(4,128)} slice(f32[8,8,128]{2,1,0:T(8,128)} %get-tuple-element.4), slice={[0:8], [0:4], [0:64]} | slice | bytes 16384 | tf_op jit(solution)/shard_map/slice | solution.py:566
  91.2 1.0 %slice_convert_fusion = f32[16,12,384]{2,1,0:T(8,128)S(1)} fusion(bf16[16,16,384]{2,1,0:T(8,128)(2,1)} %get-tuple-element.5), kind=kLoop, calls=%fused_computation | loop fusion | flops 73728 | bytes 442368 | tf_op jit(solution)/shard_map/convert_element_type | solution.py:566
  92.2 0.8 copy.12

commit v3 on v2

v3 whole, which is shorter than its diff:
```python
import functools
import math

import jax
import jax.numpy as jnp
from jax import lax
from jax.experimental import pallas as pl
from jax.experimental.pallas import tpu as pltpu
from jax.sharding import PartitionSpec as P

MESH = pl.DeviceIdType.MESH
XH, NY, NZ, NC = 2, 4, 8, 2
HEADS, SAMPLES = XH * NZ, NY * NC
D, HD, CH, LEN = 3072, 128, 64, 1024
TRIPLE = 3 * HD
BF, F32 = jnp.bfloat16, jnp.float32


def place():
    m = lax.axis_index("mp")
    return (
        lax.axis_index("grp"),
        m // (NY * NZ * NC),
        (m // (NZ * NC)) % NY,
        (m // NC) % NZ,
        m % NC,
    )


def device(g, xh, y, z, c):
    return (g, ((xh * NY + y) * NZ + z) * NC + c)


def mod(a, n):
    return lax.rem(a, n)


def rows(start, size, step):
    return pl.ds(pl.multiple_of(start, step), size)


def send(src, dst, ssem, rsem, target):
    copy = pltpu.make_async_remote_copy(
        src_ref=src, dst_ref=dst, send_sem=ssem, recv_sem=rsem, device_id=target, device_id_type=MESH
    )
    copy.start()


def take(ref, sem):
    pltpu.make_async_copy(ref, ref, sem).wait()


def greet(barrier, target):
    pl.semaphore_signal(barrier, inc=1, device_id=target, device_id_type=MESH)


Z_ORDER = (0, 1, 7, 2, 6, 3, 5, 4)


DMA = pltpu.SemaphoreType.DMA
VM = pl.BlockSpec(memory_space=pltpu.VMEM)
SM = pl.BlockSpec(memory_space=pltpu.SMEM)
HB = pl.BlockSpec(memory_space=pl.ANY)
HALF, PART = D // 2, 192
TILE = 256
SCALE = 1.0 / math.sqrt(HD)


def dot(a, b, ca=1, cb=0):
    return lax.dot_general(a, b, (((ca,), (cb,)), ((), ())), preferred_element_type=F32)


SCRATCH = dict(
    w_own=((HEADS, 24, TRIPLE), BF),
    w_in=((CH, D), BF),
    w_outT=((CH, HD), BF),
    W=((3, D, HD), BF),
    NL=((LEN, 128), BF),
    w0s=((NZ, 32, TRIPLE), BF),
    w0r=((NZ, 32, TRIPLE), BF),
    w1s=((3, NZ, 48, HD), BF),
    nst=((SAMPLES, 16, 128), BF),
    n1r=((SAMPLES, 16, 128), BF),
    nsf=((SAMPLES, 16, 128), F32),
    n1f=((32, 128), F32),
    temb=((8, D), F32),
    xf=((128, D), F32),
    xn=((LEN, D), BF),
    xnT=((D, LEN), BF),
    qkv=((LEN, TRIPLE), F32),
    qn=((LEN, HD), BF),
    kn=((LEN, HD), BF),
    v=((LEN, HD), BF),
    knT=((HD, LEN), BF),
    vT=((HD, LEN), BF),
    p32=((4, LEN, TILE), F32),
    pb=((4, LEN, TILE), BF),
    pp=((LEN // 2, 128), BF),
    p1r=((HEADS, 32, 128), BF),
    dch=((32, 128), BF),
    cot=((LEN // 2, 128), BF),
    pmine=((32, 128), F32),
    pother=((32, 128), F32),
    gs=((SAMPLES, 8, 128), F32),
    d_att=((LEN, HD), BF),
    dq=((LEN, HD), F32),
    dk=((LEN, HD), F32),
    dqk=((LEN, 2 * HD), BF),
    dv=((LEN, HD), BF),
    gr=((SAMPLES, 8, 128), F32),
    Rf=((HEADS, 16, TRIPLE), F32),
    **{
        name + str(q): (shape[:-1] + (n,), kind)
        for q, n in ((0, HD), (1, 2 * HD))
        for name, shape, kind in (
            ("T", (2, HALF, 0), BF),
            ("sibr", (2, HALF // 2, 0), BF),
            ("yst", (2, NY, XH, PART // 2, 0), BF),
            ("yr", (2, NY, XH, PART // 2, 0), BF),
            ("fin", (PART // 2, 0), F32),
            ("st", (2, XH, 8, 16, 0), BF),
            ("R", (HEADS, 16, 0), BF),
        )
    },
)
SEMS = dict(
    n1_s=None, n1_r=None, nz_s=None, nz_r=None, nx_s=None, nx_r=None, w0_s=None, w0_r=None, w_s=None,
    w1_s=3, w1_r=3, wa_r=3, wb_r=3, wr_r=3, sb_r=3, p1_s=None, p1_r=None, d_s=None, d_r=XH,
    x_s=None, x_r=None, g_s=None, g_r=None, ts_s=2, ts_r=(2, NY, 2), y_s=2,
    y_r=(2, XH, 2), f_s=2, f_r=2, in_r=3,
)
INPUTS = ("lat", "noise", "steps", "w_in_hbm", "gain", "w_qkv", "q_gain", "k_gain", "w_out")


class Refs:
    pass


def mega_kernel(*args):
    r = Refs()
    names = INPUTS + ("gen", "grad") + tuple(SCRATCH) + tuple(SEMS)
    for name, ref in zip(names, args, strict=True):
        setattr(r, name, ref)
    g, xh, y, z, c = place()
    h, me_b, X = xh * NZ + z, y * NC + c, xh * 2 + g
    fake, cross = g == 1, xh != c
    W, NL = r.W, r.NL

    def yc(dy, dc):
        return mod(y + dy, NY), mod(c + dc, NC)

    def zline(dz):
        return device(g, xh, y, mod(z + dz, NZ), c)

    def xline(dx):
        X2 = mod(X + dx, 4)
        return device(mod(X2, 2), X2 // 2, y, z, c)

    loads = (
        pltpu.make_async_copy(r.w_qkv.at[0], r.w_own, r.in_r.at[0]),
        pltpu.make_async_copy(r.w_in_hbm.at[0], r.w_in, r.in_r.at[1]),
        pltpu.make_async_copy(
            r.w_out.at[0, :, pl.ds(pl.multiple_of(h * HD, HD), HD)], r.w_outT, r.in_r.at[2]
        ),
    )
    for load in loads:
        load.start()

    barrier = pltpu.get_barrier_semaphore()
    for dy in range(NY):
        for dc in range(NC):
            if dy or dc:
                y2, c2 = yc(dy, dc)
                greet(barrier, device(g, xh, y2, z, c2))
    for dz in range(1, NZ):
        greet(barrier, zline(dz))
    for dx in range(1, 4):
        greet(barrier, xline(dx))

    @pl.when(cross)
    def _():
        for dz in range(NZ):
            greet(barrier, device(g, c, y, mod(z + dz, NZ), xh))

    loads[0].wait()
    for j in range(NZ):
        r.w0s[j, 0:24, :] = r.w_own[(1 - c) * NZ + j]
        r.w0s[j, 24:32, :] = jnp.zeros((8, TRIPLE), BF)

    rows8 = lax.broadcasted_iota(jnp.int32, (SAMPLES, 128), 0)
    ang = jnp.zeros((SAMPLES, 128), F32)
    for b in range(SAMPLES):
        ang = jnp.where(rows8 == b, r.steps[b].astype(F32), ang)
    ang = 0.5 * math.pi / 1000.0 * ang
    alpha, sigma = jnp.cos(ang), jnp.sin(ang)
    r.nsf[...] = jnp.zeros_like(r.nsf)
    for b in range(SAMPLES):
        latent = r.lat[b].astype(F32)
        noisy = alpha[b : b + 1, 0:CH] * latent + sigma[b : b + 1, 0:CH] * r.noise[b].astype(F32)
        r.nsf[b, 0:4, 0:CH] = noisy
        r.nsf[b, 0:4, CH:128] = latent
    r.nst[...] = r.nsf[...].astype(BF)

    pl.semaphore_wait(barrier, 7 + 7 + 3 + jnp.where(cross, NZ, 0))

    sib = device(g, xh, y, z, 1 - c)
    send(r.w0s, r.w0r, r.w0_s, r.w0_r, sib)
    for dy in range(NY):
        for dc in range(NC):
            y2, c2 = yc(dy, dc)
            src = r.nst.at[y2 * NC + c2]
            if dy or dc:
                send(src, r.n1r.at[me_b], r.n1_s, r.n1_r, device(g, xh, y2, z, c2))
            else:
                pltpu.make_async_copy(src, r.n1r.at[me_b], r.n1_r).start()

    take(r.w0r, r.w0_r)
    for j in range(NZ):
        mine = r.w_own[c * NZ + j].astype(F32)
        theirs = r.w0r[j, 0:24, :].astype(F32)
        low = jnp.where(c == 0, mine, theirs)
        high = jnp.where(c == 0, theirs, mine)
        both = jnp.concatenate([low, high], axis=0).astype(BF)
        for k in range(3):
            r.w1s[k, j] = both[:, k * HD : k * HD + HD]

    def to_heads(k):
        for dz in Z_ORDER:
            z2 = mod(z + dz, NZ)
            src, dst = r.w1s.at[k, z2], W.at[k, rows(((xh * NY + y) * NZ + z) * 48, 48, 48)]
            if dz:
                send(src, dst, r.w1_s.at[k], r.w1_r.at[k], device(g, c, y, z2, xh))
            else:

                @pl.when(cross)
                def _():
                    send(src, dst, r.w1_s.at[k], r.w1_r.at[k], device(g, c, y, z2, xh))

                @pl.when(jnp.logical_not(cross))
                def _():
                    pltpu.make_async_copy(src, dst, r.w1_r.at[k]).start()

    def left(k):
        take(W.at[k, 0 : 7 * 48], r.w1_s.at[k])

        @pl.when(cross)
        def _():
            take(W.at[k, 0:48], r.w1_s.at[k])

    to_heads(0)

    take(r.n1r, r.n1_r)
    for j in range(SAMPLES):
        r.n1f[j * 4 : j * 4 + 4, :] = r.n1r[j, 0:4, :].astype(F32)
    own_n = rows((X * NZ + z) * 32, 32, 32)
    NL[own_n, :] = r.n1f[...].astype(BF)
    for dz in Z_ORDER[1:]:
        send(NL.at[own_n], NL.at[own_n], r.nz_s, r.nz_r, zline(dz))

    up, down = device(g, xh, mod(y + 1, NY), z, c), device(g, xh, mod(y + 3, NY), z, c)

    def chunk(dy, k, off=0, size=2 * PART):
        return W.at[k, rows((c * NY + mod(y + dy, NY)) * 2 * PART + off, size, PART)]

    def pass_on(ref, rsem, target):
        send(ref, ref, r.w_s, rsem, target)

    def relay_own(k):
        ref = chunk(0, k)
        take(ref, r.w1_r.at[k])
        pass_on(ref, r.wa_r.at[k], up)
        pass_on(ref, r.wb_r.at[k], down)
        if k:
            pass_on(ref, r.wr_r.at[k], device(g, xh, mod(y + 2, NY), z, c))
        pass_on(ref, r.sb_r.at[k], sib)

    def relay_near(k):
        take(chunk(3, k), r.wa_r.at[k])
        if k == 0:
            pass_on(chunk(3, k, 0, PART), r.wr_r.at[k], up)
        pass_on(chunk(3, k), r.sb_r.at[k], sib)
        take(chunk(1, k), r.wb_r.at[k])
        if k == 0:
            pass_on(chunk(1, k, PART, PART), r.wr_r.at[k], down)
        pass_on(chunk(1, k), r.sb_r.at[k], sib)

    def relay_far(k):
        take(chunk(2, k), r.wr_r.at[k])
        pass_on(chunk(2, k), r.sb_r.at[k], sib)

    t_value = r.steps[me_b].astype(F32)
    index = lax.broadcasted_iota(jnp.int32, (1, D // 2), 1).astype(F32)
    phase = t_value * jnp.exp(-math.log(10000.0) * index / (D // 2))
    r.temb[0:1, 0 : D // 2] = jnp.sin(phase)
    r.temb[0:1, D // 2 :] = jnp.cos(phase)

    left(0)
    to_heads(1)
    relay_own(0)
    take(NL.at[0 : 7 * 32], r.nz_r)
    own_x = rows(X * 256, 256, 256)
    for dx in range(1, 4):
        send(NL.at[own_x], NL.at[own_x], r.nx_s, r.nx_r, xline(dx))
    left(1)
    to_heads(2)
    loads[1].wait()

    def embed(tile):
        at = rows(tile * 128, 128, 128)
        noisy = NL[at, :][:, 0:CH]
        total = jnp.zeros((128, 128), F32)
        for k in range(D // 512):
            part = dot(noisy, r.w_in[:, k * 512 : k * 512 + 512]) + r.temb[0:1, k * 512 : k * 512 + 512]
            r.xf[:, k * 512 : k * 512 + 512] = part
            sq = part * part
            for i in range(4):
                total = total + sq[:, i * 128 : i * 128 + 128]
        inv = lax.rsqrt(jnp.sum(total, axis=1, keepdims=True) * (1.0 / D) + 1e-06)
        for k in range(D // 512):
            cols = slice(k * 512, k * 512 + 512)
            done = (r.xf[:, cols] * inv * r.gain[0:1, cols]).astype(BF)
            r.xn[at, cols] = done

            @pl.when(fake)
            def _():
                r.xnT[cols, at] = done.T

    steps = {
        0: [(relay_own, 1)], 1: [(relay_near, 0)], 2: [(relay_own, 2), (relay_far, 0)],
        4: [(relay_near, 1)], 5: [(relay_far, 1)], 6: [(relay_near, 2)],
    }
    for i in range(8):
        if i == 2:
            take(NL.at[0 : 3 * 256], r.nx_r)
        embed(mod(X * 2 + i, 8))
        for step, k in steps.get(i, ()):
            step(k)

    def project(half, first, lanes, ks):
        cols = rows(half * HALF, HALF, HALF)
        weight = jnp.concatenate([W[k, cols, :] for k in ks], axis=1)
        for i in range(4):
            at = slice(i * TILE, i * TILE + TILE)
            part = dot(r.xn[at, cols], weight)
            r.qkv[at, lanes] = part if first else r.qkv[at, lanes] + part

    qk_l, v_l = slice(0, 2 * HD), slice(2 * HD, TRIPLE)
    project(c, True, qk_l, (0, 1))
    for k in range(2):
        take(W.at[k, 0:HALF], r.sb_r.at[k])
    project(1 - c, False, qk_l, (0, 1))
    relay_far(2)

    gain_q, gain_k = r.q_gain[0, pl.ds(h, 1), :], r.k_gain[0, pl.ds(h, 1), :]

    def normed(lanes):
        raw = r.qkv[:, lanes]
        inv = lax.rsqrt(jnp.mean(raw * raw, axis=-1, keepdims=True) + 1e-06)
        return raw, inv

    q_l, k_l = slice(0, HD), slice(HD, 2 * HD)
    raw, inv = normed(q_l)
    r.qn[...] = (raw * inv * gain_q).astype(BF)
    raw, inv = normed(k_l)
    k_norm = (raw * inv * gain_k).astype(BF)
    r.kn[...] = k_norm
    r.knT[...] = k_norm.T
    for t in range(4):
        at = slice(t * TILE, t * TILE + TILE)
        scores = dot(r.kn[...], r.qn[at, :], 1, 1)
        expo = jnp.exp2(scores * (SCALE * math.log2(math.e)))
        probs = expo * (1.0 / jnp.sum(expo, axis=0, keepdims=True))
        r.p32[t] = probs
        r.pb[t] = probs.astype(BF)

    project(c, True, v_l, (2,))
    take(W.at[2, 0:HALF], r.sb_r.at[2])
    project(1 - c, False, v_l, (2,))
    value = r.qkv[:, v_l].astype(BF)
    r.v[...] = value
    r.vT[...] = value.T
    loads[2].wait()

    halves = []
    for t in range(4):
        attended = dot(r.vT[...], r.pb[t]).astype(BF)
        halves.append(dot(r.w_outT[...], attended).T)
        if t % 2 == 1:
            x2 = t // 2
            r.pp[x2 * 256 : x2 * 256 + 256, :] = jnp.concatenate(halves, axis=1).astype(BF)
            halves = []
            for dz in Z_ORDER:
                z2 = mod(z + dz, NZ)
                src, dst = r.pp.at[rows((x2 * NZ + z2) * 32, 32, 32)], r.p1r.at[h]
                if dz:
                    send(src, dst, r.p1_s, r.p1_r, device(g, x2, y, z2, c))
                else:

                    @pl.when(xh == x2)
                    def _():
                        pltpu.make_async_copy(src, dst, r.p1_r).start()

                    @pl.when(xh != x2)
                    def _():
                        send(src, dst, r.p1_s, r.p1_r, device(g, x2, y, z2, c))

    take(r.p1r, r.p1_r)
    pred = jnp.sum(r.p1r[...].astype(F32), axis=0)
    r.pmine[...] = pred

    @pl.when(fake)
    def _():
        lat0 = NL[rows((xh * 2 * NZ + z) * 32, 32, 32), :].astype(F32)[:, CH:]
        lat1 = NL[rows(((xh * 2 + 1) * NZ + z) * 32, 32, 32), :].astype(F32)[:, CH:]
        latent = jnp.concatenate([lat0, lat1], axis=1)
        r.dch[...] = ((pred - latent) * (1.0 / SAMPLES)).astype(BF)
        own = rows(h * 32, 32, 32)
        for dx in range(XH):
            for dz in Z_ORDER:
                if dx or dz:
                    target = device(g, mod(xh + dx, XH), y, mod(z + dz, NZ), c)
                    send(r.dch, r.cot.at[own], r.d_s, r.d_r.at[xh], target)
        pltpu.make_async_copy(r.dch, r.cot.at[own], r.d_r.at[xh]).start()

    partner = device(1 - g, xh, y, z, c)
    send(r.pmine, r.pother, r.x_s, r.x_r, partner)

    def generator():
        take(r.pother, r.x_r)
        diff = jnp.where(g == 0, r.pother[...] - r.pmine[...], r.pmine[...] - r.pother[...])
        mine = jnp.where(g == 0, diff[:, 0:CH], diff[:, CH:])
        for j in range(SAMPLES):
            r.gs[j, 0:4, 0:CH] = mine[j * 4 : j * 4 + 4, :]
        for dy in range(NY):
            for dc in range(NC):
                y2, c2 = yc(dy, dc)
                src, dst = r.gs.at[y2 * NC + c2], r.gr.at[me_b]
                if dy or dc:
                    send(src, dst, r.g_s, r.g_r, device(g, xh, y2, z, c2))
                else:
                    pltpu.make_async_copy(src, dst, r.g_r).start()

    def deliver(q, zh, slot, net, x2, head):
        yr, fin, st, R = (getattr(r, name + str(q)) for name in ("yr", "fin", "st", "R"))
        take(yr.at[zh, :, slot], r.y_r.at[q, slot, zh])
        fin[...] = jnp.sum(yr[zh, :, slot].astype(F32), axis=0)
        for i in range(8):
            st[zh, slot, i, 0:12, :] = fin[i * 12 : i * 12 + 12, :].astype(BF)
        fs, fr = r.f_s.at[q], r.f_r.at[q]
        for e in range(4):
            zq, zr = mod(z // 4 + e // 2, 2), mod(z + e, 2)
            z2 = zq * 4 + zh * 2 + zr
            for c2 in range(NC):
                src, dst = st.at[zh, slot, (zq * 2 + zr) * NC + c2], R.at[head]
                target = device(net, x2, y, z2, c2)
                if e:
                    send(src, dst, fs, fr, target)
                else:
                    me = (x2 == xh) & (c2 == c) & (z2 == z)

                    @pl.when(me)
                    def _():
                        pltpu.make_async_copy(src, dst, fr).start()

                    @pl.when(jnp.logical_not(me))
                    def _():
                        send(src, dst, fs, fr, target)


    @pl.when(jnp.logical_not(fake))
    def _():
        generator()
        for q in range(2):
            for zh in range(2):
                deliver(q, zh, 0, 0, xh, c * NZ + z)
        for q in range(2):
            take(getattr(r, f"R{q}").at[0:15], r.f_s.at[q])

    @pl.when(fake)
    def _():
        for t in range(4):
            if t % 2 == 0:
                take(r.cot.at[0:256], r.d_r.at[t // 2])
            at = slice(t * TILE, t * TILE + TILE)
            cot = r.cot[(t // 2) * 256 : (t // 2) * 256 + 256, (t % 2) * CH : (t % 2) * CH + CH]
            r.d_att[at, :] = dot(cot, r.w_outT[...]).astype(BF)
        dv = dot(r.pb[0], r.d_att[0:TILE, :])
        for t in range(1, 4):
            dv = dv + dot(r.pb[t], r.d_att[t * TILE : t * TILE + TILE, :])
        r.dv[...] = dv.astype(BF)

        def scores_back(t):
            at = slice(t * TILE, t * TILE + TILE)
            d_probs = dot(r.v[...], r.d_att[at, :], 1, 1)
            probs = r.p32[t]
            mean = jnp.sum(probs * d_probs, axis=0, keepdims=True)
            d_score = (probs * (d_probs - mean)).astype(BF)
            dk = dot(d_score, r.qn[at, :])
            if t:
                r.dk[...] += dk
            else:
                r.dk[...] = dk
            r.dq[at, :] = dot(r.knT[...], d_score).T

        def unnorm(lanes, gain, grad):
            raw, inv = normed(lanes)
            scaled = grad * SCALE * gain
            unit = raw * inv
            inner = jnp.mean(unit * scaled, axis=-1, keepdims=True)
            r.dqk[:, lanes] = (inv * (scaled - unit * inner)).astype(BF)

        def place_of(j, x2):
            return (x2 * NY + mod(y + j, NY)) * (PART // 2)

        class Lanes:
            def __init__(self, q, grad):
                self.q, self.grad = q, grad
                for name in ("T", "sibr", "yst", "yr", "R"):
                    setattr(self, name, getattr(r, name + str(q)))

            def block(self, half, zh, js):
                pairs = [(j, x2) for j in js for x2 in range(XH)]
                left = []
                for j, x2 in pairs:
                    first = half * HALF + (x2 * NY + mod(y + j, NY)) * PART + zh * 48
                    left += [r.xnT[rows(first + zq * 96, 48, 48), :] for zq in range(2)]
                out = dot(jnp.concatenate(left, axis=0), self.grad[...]).astype(BF)
                for i, (j, x2) in enumerate(pairs):
                    at = rows(half * (HALF // 2) + place_of(j, x2), 96, 96)
                    self.T[zh, at, :] = out[i * 96 : i * 96 + 96]

            def to_sibling(self, zh, js):
                self.block(1 - c, zh, js)
                for j in js:
                    for x2 in range(XH):
                        src = self.T.at[zh, rows((1 - c) * (HALF // 2) + place_of(j, x2), 96, 96)]
                        dst = self.sibr.at[zh, rows(place_of(j, x2), 96, 96)]
                        send(src, dst, r.ts_s.at[self.q], r.ts_r.at[self.q, j, zh], sib)

            def chunks_out(self, zh, js):
                ys = r.y_s.at[self.q]
                for j in js:
                    take(self.sibr.at[zh, 0:PART], r.ts_r.at[self.q, j, zh])
                    for x2 in range(XH):
                        mine = self.T[zh, rows(c * (HALF // 2) + place_of(j, x2), 96, 96), :]
                        theirs = self.sibr[zh, rows(place_of(j, x2), 96, 96), :]
                        src = self.yst.at[zh, j, x2]
                        src[...] = (mine.astype(F32) + theirs.astype(F32)).astype(BF)

                        @pl.when(c == 0)
                        def _():
                            target = device(0, x2, mod(y + j, NY), z, xh)
                            send(src, self.yr.at[zh, j, 0], ys, r.y_r.at[self.q, 0, zh], target)

                        @pl.when(c == 1)
                        def _():
                            dst, arrive = self.yr.at[zh, j, x2], r.y_r.at[self.q, x2, zh]
                            if j:
                                send(src, dst, ys, arrive, device(1, xh, mod(y + j, NY), z, 1))
                            else:
                                pltpu.make_async_copy(src, dst, arrive).start()

            def drain(self):
                take(self.sibr, r.ts_s.at[self.q])
                take(self.yst.at[:, 0:3], r.y_s.at[self.q])

                @pl.when(c == 0)
                def _():
                    take(self.yst.at[:, 3], r.y_s.at[self.q])

        a, b = Lanes(0, r.dv), Lanes(1, r.dqk)
        near, rest = (2, 1), (3, 0)
        a.to_sibling(0, near)
        a.to_sibling(0, rest)
        a.block(c, 0, near)
        a.block(c, 0, rest)
        a.chunks_out(0, near)
        a.to_sibling(1, near)
        a.to_sibling(1, rest)
        a.chunks_out(0, rest)
        a.block(c, 1, near)
        a.block(c, 1, rest)
        a.chunks_out(1, near + rest)
        for t in range(4):
            scores_back(t)
        unnorm(q_l, gain_q, r.dq[...])
        unnorm(k_l, gain_k, r.dk[...])
        b.to_sibling(0, near)
        b.to_sibling(0, rest)
        b.block(c, 0, near)
        b.block(c, 0, rest)
        b.chunks_out(0, near)
        b.to_sibling(1, near)
        b.chunks_out(0, rest)
        b.to_sibling(1, rest)
        b.block(c, 1, near)
        b.block(c, 1, rest)
        b.chunks_out(1, near + rest)
        generator()

        @pl.when(c == 1)
        def _():
            for q in range(2):
                for zh in range(2):
                    for x2 in range(XH):
                        deliver(q, zh, x2, 1, x2, h)
            for R, fs in ((r.R0, r.f_s.at[0]), (r.R1, r.f_s.at[1])):
                take(R, fs)
                take(R.at[0:15], fs)

        a.drain()
        b.drain()
        take(r.cot.at[0 : 15 * 32], r.d_s)

    take(r.n1r.at[0:7], r.n1_s)
    take(r.w0s, r.w0_s)
    take(NL.at[0 : 7 * 32], r.nz_s)
    take(NL.at[0 : 3 * 256], r.nx_s)
    for k in range(3):
        if k == 2:
            left(2)
        take(W.at[k, 0 : 7 * 2 * PART], r.w_s)

    take(r.p1r.at[0:15], r.p1_s)
    take(r.pmine, r.x_s)
    take(r.gr.at[0:7], r.g_s)
    take(r.gr, r.g_r)
    r.gen[...] = r.gr[:, 0:4, 0:CH]
    take(r.R0, r.f_r.at[0])
    r.Rf[:, :, v_l] = r.R0[...].astype(F32)
    take(r.R1, r.f_r.at[1])
    r.Rf[:, :, qk_l] = r.R1[...].astype(F32)
    for i in range(12):
        r.grad[i] = r.Rf[:, i, :]


def on_device(latents, noise, steps_t, w_in, norm_gain, w_qkv, q_gain, k_gain, w_out):
    gen, grads = pl.pallas_call(
        mega_kernel,
        out_shape=(
            jax.ShapeDtypeStruct((SAMPLES, 4, CH), F32),
            jax.ShapeDtypeStruct((12, HEADS, TRIPLE), F32),
        ),
        in_specs=[VM, VM, SM, HB, VM, HB, VM, VM, HB],
        out_specs=(VM, VM),
        scratch_shapes=[pltpu.VMEM(*spec) for spec in SCRATCH.values()]
        + [DMA if n is None else DMA(n if isinstance(n, tuple) else (n,)) for n in SEMS.values()],
        compiler_params=pltpu.CompilerParams(
            collective_id=0, has_side_effects=True, vmem_limit_bytes=58 * 1024 * 1024
        ),
        name="distill_step",
    )(latents, noise, steps_t, w_in, norm_gain, w_qkv, q_gain, k_gain, w_out.transpose(0, 2, 1))
    return gen, grads.transpose(1, 0, 2)


def solution(mesh):
    return jax.shard_map(
        on_device,
        mesh=mesh,
        in_specs=(
            P(None, ("grp", "mp"), None),
            P(None, ("grp", "mp"), None),
            P(),
            P("grp", None, None),
            P("grp", None),
            P("grp", None, "mp", None),
            P("grp", None, None),
            P("grp", None, None),
            P("grp", None, None),
        ),
        out_specs=(P(None, ("grp", "mp"), None), P(None, ("grp", "mp"), None)),
        check_vma=False,
    )
```

time: 93.2 us -> 85.1 us (0.913)
  the two profiles are of different devices: /device:TPU:7 before, /device:TPU:1 now
where the time goes in v3:
time: 85.1 us; the launch traced here: 84.8 us
  Pallas kernels  81.2 us (95%)
  local copies, waits for them, and re-layouts  3.02 us (4%)
    pallas_call x1, Pallas kernels, on_device(): pl.pallas_call(mega_kernel, out_shape=(jax.ShapeDtypeStruct((SAMPLES, 4,...  81.2 us
    unnamed x2, local copies, waits for them, and re-layouts  3.02 us

profile of v3, /device:TPU:1, one launch (start us, length us, event | category | flops | bytes accessed | tf_op | source)
XLA Modules:
  0.0 84.8 jit_solution(6808114136693208648)
XLA Ops:
  0.6 81.2 %distill_step.1 = (f32[8,4,64]{2,1,0:T(4,128)}, f32[12,16,384]{2,1,0:T(8,128)}) custom-call(bf16[8,4,64]{2,1,0:T(4,128)(2,1)} %args_0_.4, bf16[8,4,64]{2,1,0:T(4,128)(2,1)} %args_1_.4, s32[8]{0:T(128)} %args_2_.4, bf16[1,64,3072]{2,1,0:T(8,128)(2,1)} %args_3_.4, f32[1,3072]{1,0:T(1,128)} %args_4_.4, bf16[1,16,24,384]{3,2,1,0:T(8,128)(2,1)} %args_5_.4, ...), custom_call_target="tpu_custom_call" | custom-call | tf_op jit(solution)/shard_map/distill_step/pallas_call | solution.py:638
  81.8 1.3 %copy.13 = f32[8,4,64]{2,1,0:T(4,128)} copy(f32[8,4,64]{2,1,0:T(4,128)} %get-tuple-element.8) | data formatting | bytes 16384
  83.1 1.7 %copy.14 = f32[16,12,384]{2,0,1:T(8,128)} copy(f32[16,12,384]{2,0,1:T(8,128)} %bitcast.2) | data formatting | bytes 589824

commit v4 on v3

--- a/solution.py
+++ b/solution.py
@@ -71,6 +71,11 @@
 
 
 SCRATCH = dict(
+    lat=((SAMPLES, 4, CH), BF),
+    noise=((SAMPLES, 4, CH), BF),
+    gain=((1, D), F32),
+    q_gain=((1, HEADS, HD), F32),
+    k_gain=((1, HEADS, HD), F32),
     w_own=((HEADS, 24, TRIPLE), BF),
     w_in=((CH, D), BF),
     w_outT=((CH, HD), BF),
@@ -127,9 +132,11 @@
     n1_s=None, n1_r=None, nz_s=None, nz_r=None, nx_s=None, nx_r=None, w0_s=None, w0_r=None, w_s=None,
     w1_s=3, w1_r=3, wa_r=3, wb_r=3, wr_r=3, sb_r=3, p1_s=None, p1_r=None, d_s=None, d_r=XH,
     x_s=None, x_r=None, g_s=None, g_r=None, ts_s=2, ts_r=(2, NY, 2), y_s=2,
-    y_r=(2, XH, 2), f_s=2, f_r=2, in_r=3,
+    y_r=(2, XH, 2), f_s=2, f_r=2, in_r=8,
 )
-INPUTS = ("lat", "noise", "steps", "w_in_hbm", "gain", "w_qkv", "q_gain", "k_gain", "w_out")
+INPUTS = (
+    "lat_hbm", "noise_hbm", "steps", "w_in_hbm", "gain_hbm", "w_qkv", "q_gain_hbm", "k_gain_hbm", "w_out"
+)
 
 
 class Refs:
@@ -155,16 +162,6 @@
     def xline(dx):
         X2 = mod(X + dx, 4)
         return device(mod(X2, 2), X2 // 2, y, z, c)
-
-    loads = (
-        pltpu.make_async_copy(r.w_qkv.at[0], r.w_own, r.in_r.at[0]),
-        pltpu.make_async_copy(r.w_in_hbm.at[0], r.w_in, r.in_r.at[1]),
-        pltpu.make_async_copy(
-            r.w_out.at[0, :, pl.ds(pl.multiple_of(h * HD, HD), HD)], r.w_outT, r.in_r.at[2]
-        ),
-    )
-    for load in loads:
-        load.start()
 
     barrier = pltpu.get_barrier_semaphore()
     for dy in range(NY):
@@ -182,11 +179,28 @@
         for dz in range(NZ):
             greet(barrier, device(g, c, y, mod(z + dz, NZ), xh))
 
+    loads = (
+        pltpu.make_async_copy(r.w_qkv.at[0], r.w_own, r.in_r.at[0]),
+        pltpu.make_async_copy(r.w_in_hbm.at[0], r.w_in, r.in_r.at[1]),
+        pltpu.make_async_copy(
+            r.w_out.at[0, :, pl.ds(pl.multiple_of(h * HD, HD), HD)], r.w_outT, r.in_r.at[2]
+        ),
+        pltpu.make_async_copy(r.lat_hbm, r.lat, r.in_r.at[3]),
+        pltpu.make_async_copy(r.noise_hbm, r.noise, r.in_r.at[4]),
+        pltpu.make_async_copy(r.gain_hbm, r.gain, r.in_r.at[5]),
+        pltpu.make_async_copy(r.q_gain_hbm, r.q_gain, r.in_r.at[6]),
+        pltpu.make_async_copy(r.k_gain_hbm, r.k_gain, r.in_r.at[7]),
+    )
+    for load in loads:
+        load.start()
+
     loads[0].wait()
     for j in range(NZ):
         r.w0s[j, 0:24, :] = r.w_own[(1 - c) * NZ + j]
         r.w0s[j, 24:32, :] = jnp.zeros((8, TRIPLE), BF)
 
+    loads[3].wait()
+    loads[4].wait()
     rows8 = lax.broadcasted_iota(jnp.int32, (SAMPLES, 128), 0)
     ang = jnp.zeros((SAMPLES, 128), F32)
     for b in range(SAMPLES):
@@ -194,6 +208,7 @@
     ang = 0.5 * math.pi / 1000.0 * ang
     alpha, sigma = jnp.cos(ang), jnp.sin(ang)
     r.nsf[...] = jnp.zeros_like(r.nsf)
+    r.gs[...] = jnp.zeros_like(r.gs)
     for b in range(SAMPLES):
         latent = r.lat[b].astype(F32)
         noisy = alpha[b : b + 1, 0:CH] * latent + sigma[b : b + 1, 0:CH] * r.noise[b].astype(F32)
@@ -303,7 +318,8 @@
         send(NL.at[own_x], NL.at[own_x], r.nx_s, r.nx_r, xline(dx))
     left(1)
     to_heads(2)
-    loads[1].wait()
+    for i in (1, 5, 6, 7):
+        loads[i].wait()
 
     def embed(tile):
         at = rows(tile * 128, 128, 128)
@@ -470,7 +486,7 @@
     @pl.when(jnp.logical_not(fake))
     def _():
         generator()
-        for q in range(2):
+        for q in (1, 0):
             for zh in range(2):
                 deliver(q, zh, 0, 0, xh, c * NZ + z)
         for q in range(2):
@@ -484,11 +500,6 @@
             at = slice(t * TILE, t * TILE + TILE)
             cot = r.cot[(t // 2) * 256 : (t // 2) * 256 + 256, (t % 2) * CH : (t % 2) * CH + CH]
             r.d_att[at, :] = dot(cot, r.w_outT[...]).astype(BF)
-        dv = dot(r.pb[0], r.d_att[0:TILE, :])
-        for t in range(1, 4):
-            dv = dv + dot(r.pb[t], r.d_att[t * TILE : t * TILE + TILE, :])
-        r.dv[...] = dv.astype(BF)
-
         def scores_back(t):
             at = slice(t * TILE, t * TILE + TILE)
             d_probs = dot(r.v[...], r.d_att[at, :], 1, 1)
@@ -570,17 +581,6 @@
 
         a, b = Lanes(0, r.dv), Lanes(1, r.dqk)
         near, rest = (2, 1), (3, 0)
-        a.to_sibling(0, near)
-        a.to_sibling(0, rest)
-        a.block(c, 0, near)
-        a.block(c, 0, rest)
-        a.chunks_out(0, near)
-        a.to_sibling(1, near)
-        a.to_sibling(1, rest)
-        a.chunks_out(0, rest)
-        a.block(c, 1, near)
-        a.block(c, 1, rest)
-        a.chunks_out(1, near + rest)
         for t in range(4):
             scores_back(t)
         unnorm(q_l, gain_q, r.dq[...])
@@ -596,11 +596,26 @@
         b.block(c, 1, near)
         b.block(c, 1, rest)
         b.chunks_out(1, near + rest)
+        dv = dot(r.pb[0], r.d_att[0:TILE, :])
+        for t in range(1, 4):
+            dv = dv + dot(r.pb[t], r.d_att[t * TILE : t * TILE + TILE, :])
+        r.dv[...] = dv.astype(BF)
+        a.to_sibling(0, near)
+        a.to_sibling(0, rest)
+        a.block(c, 0, near)
+        a.block(c, 0, rest)
+        a.chunks_out(0, near)
+        a.to_sibling(1, near)
+        a.to_sibling(1, rest)
+        a.chunks_out(0, rest)
+        a.block(c, 1, near)
+        a.block(c, 1, rest)
+        a.chunks_out(1, near + rest)
         generator()
 
         @pl.when(c == 1)
         def _():
-            for q in range(2):
+            for q in (1, 0):
                 for zh in range(2):
                     for x2 in range(XH):
                         deliver(q, zh, x2, 1, x2, h)
@@ -625,23 +640,24 @@
     take(r.pmine, r.x_s)
     take(r.gr.at[0:7], r.g_s)
     take(r.gr, r.g_r)
-    r.gen[...] = r.gr[:, 0:4, 0:CH]
+    for b in range(SAMPLES):
+        r.gen[b * 4 : b * 4 + 4, :] = r.gr[b, 0:4, :]
     take(r.R0, r.f_r.at[0])
     r.Rf[:, :, v_l] = r.R0[...].astype(F32)
     take(r.R1, r.f_r.at[1])
     r.Rf[:, :, qk_l] = r.R1[...].astype(F32)
     for i in range(12):
-        r.grad[i] = r.Rf[:, i, :]
+        r.grad[i * HEADS : i * HEADS + HEADS, :] = r.Rf[:, i, :].astype(BF)
 
 
 def on_device(latents, noise, steps_t, w_in, norm_gain, w_qkv, q_gain, k_gain, w_out):
     gen, grads = pl.pallas_call(
         mega_kernel,
         out_shape=(
-            jax.ShapeDtypeStruct((SAMPLES, 4, CH), F32),
-            jax.ShapeDtypeStruct((12, HEADS, TRIPLE), F32),
+            jax.ShapeDtypeStruct((SAMPLES * 4, 128), F32),
+            jax.ShapeDtypeStruct((12 * HEADS, TRIPLE), BF),
         ),
-        in_specs=[VM, VM, SM, HB, VM, HB, VM, VM, HB],
+        in_specs=[HB, HB, SM, HB, HB, HB, HB, HB, HB],
         out_specs=(VM, VM),
         scratch_shapes=[pltpu.VMEM(*spec) for spec in SCRATCH.values()]
         + [DMA if n is None else DMA(n if isinstance(n, tuple) else (n,)) for n in SEMS.values()],
@@ -650,7 +666,8 @@
         ),
         name="distill_step",
     )(latents, noise, steps_t, w_in, norm_gain, w_qkv, q_gain, k_gain, w_out.transpose(0, 2, 1))
-    return gen, grads.transpose(1, 0, 2)
+    grads = grads.astype(F32).reshape(12, HEADS, TRIPLE).transpose(1, 0, 2)
+    return gen[:, :CH].reshape(SAMPLES, 4, CH), grads
 
 
 def solution(mesh):

time: 85.1 us -> 83.2 us (0.978)
  local copies, waits for them, and re-layouts: 3.02 us -> 0.61 us
  other arithmetic: 0 us -> 1.65 us
  Pallas kernels: 81.2 us -> 80.1 us
    unnamed x2 -> x3, local copies, waits for them, and re-layouts: 3.02 us -> 0.61 us
    transpose x0 -> x1, other arithmetic: none -> 1.65 us  [on_device(): grads = grads.astype(F32).reshape(12, HEADS, TRIPLE).transpose(1, 0, 2)]
    pallas_call x1, Pallas kernels: 81.2 us -> 80.1 us  [on_device(): pl.pallas_call(mega_kernel, out_shape=(jax.ShapeDtypeStruct((SAMPLES * 4,...]
where the time goes in v4:
time: 83.2 us; the launch traced here: 83 us
  Pallas kernels  80.1 us (96%)
  other arithmetic  1.65 us (2%)
    pallas_call x1, Pallas kernels, on_device(): pl.pallas_call(mega_kernel, out_shape=(jax.ShapeDtypeStruct((SAMPLES * 4,...  80.1 us

profile of v4, /device:TPU:1, one launch (start us, length us, event | category | flops | bytes accessed | tf_op | source)
XLA Modules:
  0.0 83.0 jit_solution(14633928192093190633)
XLA Ops:
  0.6 80.1 %distill_step.1 = (f32[32,128]{1,0:T(8,128)}, bf16[192,384]{1,0:T(8,128)(2,1)}) custom-call(bf16[8,4,64]{2,1,0:T(4,128)(2,1)} %args_0_.4, bf16[8,4,64]{2,1,0:T(4,128)(2,1)} %args_1_.4, s32[8]{0:T(128)} %args_2_.4, bf16[1,64,3072]{2,1,0:T(8,128)(2,1)} %args_3_.4, f32[1,3072]{1,0:T(1,128)} %args_4_.4, bf16[1,16,24,384]{3,2,1,0:T(8,128)(2,1)} %args_5_.4, ...), custom_call_target="tpu_custom_call" | custom-call | tf_op jit(solution)/shard_map/distill_step/pallas_call | solution.py:654
  80.8 0.0 copy-start
  80.8 1.6 %convert_bitcast_fusion = f32[16,12,384]{2,0,1:T(8,128)} fusion(bf16[12,16,384]{2,1,0:T(8,128)(2,1)} %bitcast.8), kind=kLoop, calls=%fused_computation | loop fusion | flops 73728 | bytes 442368 | tf_op jit(solution)/shard_map/transpose | solution.py:669
  82.4 0.0 copy-done
  82.4 0.6 copy.12
Async XLA Ops:
  80.8 1.7 %copy-start = (f32[32,128]{1,0:T(8,128)S(1)}, f32[32,128]{1,0:T(8,128)}, u32[]{:S(2)}) copy-start(f32[32,128]{1,0:T(8,128)} %get-tuple-element.4) | copy-start | bytes 49156

commit v5 on v4

--- a/solution.py
+++ b/solution.py
@@ -64,6 +64,7 @@
 HALF, PART = D // 2, 192
 TILE = 256
 SCALE = 1.0 / math.sqrt(HD)
+FAR_FIRST = (4, 3, 5, 2, 6, 1, 7, 0)
 
 
 def dot(a, b, ca=1, cb=0):
@@ -130,7 +131,7 @@
 )
 SEMS = dict(
     n1_s=None, n1_r=None, nz_s=None, nz_r=None, nx_s=None, nx_r=None, w0_s=None, w0_r=None, w_s=None,
-    w1_s=3, w1_r=3, wa_r=3, wb_r=3, wr_r=3, sb_r=3, p1_s=None, p1_r=None, d_s=None, d_r=XH,
+    w1_s=3, w1_r=3, wa_r=3, wb_r=3, wr_r=3, sb_r=(3, 2), p1_s=None, p1_r=None, d_s=None, d_r=XH,
     x_s=None, x_r=None, g_s=None, g_r=None, ts_s=2, ts_r=(2, NY, 2), y_s=2,
     y_r=(2, XH, 2), f_s=2, f_r=2, in_r=8,
 )
@@ -269,7 +270,7 @@
         r.n1f[j * 4 : j * 4 + 4, :] = r.n1r[j, 0:4, :].astype(F32)
     own_n = rows((X * NZ + z) * 32, 32, 32)
     NL[own_n, :] = r.n1f[...].astype(BF)
-    for dz in Z_ORDER[1:]:
+    for dz in FAR_FIRST[:7]:
         send(NL.at[own_n], NL.at[own_n], r.nz_s, r.nz_r, zline(dz))
 
     up, down = device(g, xh, mod(y + 1, NY), z, c), device(g, xh, mod(y + 3, NY), z, c)
@@ -287,21 +288,21 @@
         pass_on(ref, r.wb_r.at[k], down)
         if k:
             pass_on(ref, r.wr_r.at[k], device(g, xh, mod(y + 2, NY), z, c))
-        pass_on(ref, r.sb_r.at[k], sib)
+        pass_on(ref, r.sb_r.at[k, 0], sib)
 
     def relay_near(k):
         take(chunk(3, k), r.wa_r.at[k])
         if k == 0:
             pass_on(chunk(3, k, 0, PART), r.wr_r.at[k], up)
-        pass_on(chunk(3, k), r.sb_r.at[k], sib)
+        pass_on(chunk(3, k), r.sb_r.at[k, 0], sib)
         take(chunk(1, k), r.wb_r.at[k])
         if k == 0:
             pass_on(chunk(1, k, PART, PART), r.wr_r.at[k], down)
-        pass_on(chunk(1, k), r.sb_r.at[k], sib)
+        pass_on(chunk(1, k), r.sb_r.at[k, 0], sib)
 
     def relay_far(k):
         take(chunk(2, k), r.wr_r.at[k])
-        pass_on(chunk(2, k), r.sb_r.at[k], sib)
+        pass_on(chunk(2, k), r.sb_r.at[k, 1], sib)
 
     t_value = r.steps[me_b].astype(F32)
     index = lax.broadcasted_iota(jnp.int32, (1, D // 2), 1).astype(F32)
@@ -363,7 +364,8 @@
     qk_l, v_l = slice(0, 2 * HD), slice(2 * HD, TRIPLE)
     project(c, True, qk_l, (0, 1))
     for k in range(2):
-        take(W.at[k, 0:HALF], r.sb_r.at[k])
+        take(W.at[k, 0 : 6 * PART], r.sb_r.at[k, 0])
+        take(W.at[k, 0 : 2 * PART], r.sb_r.at[k, 1])
     project(1 - c, False, qk_l, (0, 1))
     relay_far(2)
 
@@ -390,8 +392,18 @@
         r.pb[t] = probs.astype(BF)
 
     project(c, True, v_l, (2,))
-    take(W.at[2, 0:HALF], r.sb_r.at[2])
-    project(1 - c, False, v_l, (2,))
+
+    def project_v(dy):
+        cols = rows(((1 - c) * NY + mod(y + dy, NY)) * 2 * PART, 2 * PART, 2 * PART)
+        for i in range(4):
+            at = slice(i * TILE, i * TILE + TILE)
+            r.qkv[at, v_l] += dot(r.xn[at, cols], W[2, cols, :])
+
+    take(W.at[2, 0 : 6 * PART], r.sb_r.at[2, 0])
+    for dy in (0, 3, 1):
+        project_v(dy)
+    take(W.at[2, 0 : 2 * PART], r.sb_r.at[2, 1])
+    project_v(2)
     value = r.qkv[:, v_l].astype(BF)
     r.v[...] = value
     r.vT[...] = value.T
@@ -405,7 +417,7 @@
             x2 = t // 2
             r.pp[x2 * 256 : x2 * 256 + 256, :] = jnp.concatenate(halves, axis=1).astype(BF)
             halves = []
-            for dz in Z_ORDER:
+            for dz in FAR_FIRST:
                 z2 = mod(z + dz, NZ)
                 src, dst = r.pp.at[rows((x2 * NZ + z2) * 32, 32, 32)], r.p1r.at[h]
                 if dz:
@@ -431,8 +443,8 @@
         latent = jnp.concatenate([lat0, lat1], axis=1)
         r.dch[...] = ((pred - latent) * (1.0 / SAMPLES)).astype(BF)
         own = rows(h * 32, 32, 32)
-        for dx in range(XH):
-            for dz in Z_ORDER:
+        for dx in (1, 0):
+            for dz in FAR_FIRST:
                 if dx or dz:
                     target = device(g, mod(xh + dx, XH), y, mod(z + dz, NZ), c)
                     send(r.dch, r.cot.at[own], r.d_s, r.d_r.at[xh], target)
@@ -463,7 +475,7 @@
         for i in range(8):
             st[zh, slot, i, 0:12, :] = fin[i * 12 : i * 12 + 12, :].astype(BF)
         fs, fr = r.f_s.at[q], r.f_r.at[q]
-        for e in range(4):
+        for e in (3, 2, 1, 0):
             zq, zr = mod(z // 4 + e // 2, 2), mod(z + e, 2)
             z2 = zq * 4 + zh * 2 + zr
             for c2 in range(NC):
@@ -494,20 +506,20 @@
 
     @pl.when(fake)
     def _():
-        for t in range(4):
-            if t % 2 == 0:
-                take(r.cot.at[0:256], r.d_r.at[t // 2])
-            at = slice(t * TILE, t * TILE + TILE)
-            cot = r.cot[(t // 2) * 256 : (t // 2) * 256 + 256, (t % 2) * CH : (t % 2) * CH + CH]
+        def scores_back(i):
+            x2 = mod(xh + i // 2, XH)
+            if i % 2 == 0:
+                take(r.cot.at[0:256], r.d_r.at[x2])
+            t = x2 * 2 + i % 2
+            at = rows(t * TILE, TILE, TILE)
+            cot = r.cot[rows(x2 * 256, 256, 256), (i % 2) * CH : (i % 2) * CH + CH]
             r.d_att[at, :] = dot(cot, r.w_outT[...]).astype(BF)
-        def scores_back(t):
-            at = slice(t * TILE, t * TILE + TILE)
             d_probs = dot(r.v[...], r.d_att[at, :], 1, 1)
             probs = r.p32[t]
             mean = jnp.sum(probs * d_probs, axis=0, keepdims=True)
             d_score = (probs * (d_probs - mean)).astype(BF)
             dk = dot(d_score, r.qn[at, :])
-            if t:
+            if i:
                 r.dk[...] += dk
             else:
                 r.dk[...] = dk

time: 83.2 us -> 82 us (0.986)
  Pallas kernels: 80.1 us -> 78.9 us
    pallas_call x1, Pallas kernels: 80.1 us -> 78.9 us  [on_device(): pl.pallas_call(mega_kernel, out_shape=(jax.ShapeDtypeStruct((SAMPLES * 4,...]
where the time goes in v5:
time: 82 us; the launch traced here: 81.9 us
  Pallas kernels  78.9 us (96%)
  other arithmetic  1.65 us (2%)
    pallas_call x1, Pallas kernels, on_device(): pl.pallas_call(mega_kernel, out_shape=(jax.ShapeDtypeStruct((SAMPLES * 4,...  78.9 us
    transpose x1, other arithmetic, on_device(): grads = grads.astype(F32).reshape(12, HEADS, TRIPLE).transpose(1, 0, 2)  1.65 us

profile of v5, /device:TPU:1, one launch (start us, length us, event | category | flops | bytes accessed | tf_op | source)
XLA Modules:
  0.0 81.9 jit_solution(6205080226475911906)
XLA Ops:
  0.6 78.9 %distill_step.1 = (f32[32,128]{1,0:T(8,128)}, bf16[192,384]{1,0:T(8,128)(2,1)}) custom-call(bf16[8,4,64]{2,1,0:T(4,128)(2,1)} %args_0_.4, bf16[8,4,64]{2,1,0:T(4,128)(2,1)} %args_1_.4, s32[8]{0:T(128)} %args_2_.4, bf16[1,64,3072]{2,1,0:T(8,128)(2,1)} %args_3_.4, f32[1,3072]{1,0:T(1,128)} %args_4_.4, bf16[1,16,24,384]{3,2,1,0:T(8,128)(2,1)} %args_5_.4, ...), custom_call_target="tpu_custom_call" | custom-call | tf_op jit(solution)/shard_map/distill_step/pallas_call | solution.py:666
  79.6 0.0 copy-start
  79.6 1.6 %convert_bitcast_fusion = f32[16,12,384]{2,0,1:T(8,128)} fusion(bf16[12,16,384]{2,1,0:T(8,128)(2,1)} %bitcast.8), kind=kLoop, calls=%fused_computation | loop fusion | flops 73728 | bytes 442368 | tf_op jit(solution)/shard_map/transpose | solution.py:681
  81.2 0.0 copy-done
  81.2 0.6 copy.12
Async XLA Ops:
  79.6 1.7 %copy-start = (f32[32,128]{1,0:T(8,128)S(1)}, f32[32,128]{1,0:T(8,128)}, u32[]{:S(2)}) copy-start(f32[32,128]{1,0:T(8,128)} %get-tuple-element.4) | copy-start | bytes 49156

commit v6 on v5

--- a/solution.py
+++ b/solution.py
@@ -241,7 +241,7 @@
             r.w1s[k, j] = both[:, k * HD : k * HD + HD]
 
     def to_heads(k):
-        for dz in Z_ORDER:
+        for dz in FAR_FIRST:
             z2 = mod(z + dz, NZ)
             src, dst = r.w1s.at[k, z2], W.at[k, rows(((xh * NY + y) * NZ + z) * 48, 48, 48)]
             if dz:
@@ -315,7 +315,7 @@
     relay_own(0)
     take(NL.at[0 : 7 * 32], r.nz_r)
     own_x = rows(X * 256, 256, 256)
-    for dx in range(1, 4):
+    for dx in (2, 1, 3):
         send(NL.at[own_x], NL.at[own_x], r.nx_s, r.nx_r, xline(dx))
     left(1)
     to_heads(2)

time: 82 us -> 80.2 us (0.978)
  Pallas kernels: 78.9 us -> 77.2 us
    pallas_call x1, Pallas kernels: 78.9 us -> 77.2 us  [on_device(): pl.pallas_call(mega_kernel, out_shape=(jax.ShapeDtypeStruct((SAMPLES * 4,...]
where the time goes in v6:
time: 80.2 us; the launch traced here: 80.1 us
  Pallas kernels  77.2 us (96%)
  other arithmetic  1.65 us (2%)
    pallas_call x1, Pallas kernels, on_device(): pl.pallas_call(mega_kernel, out_shape=(jax.ShapeDtypeStruct((SAMPLES * 4,...  77.2 us
    transpose x1, other arithmetic, on_device(): grads = grads.astype(F32).reshape(12, HEADS, TRIPLE).transpose(1, 0, 2)  1.65 us

profile of v6, /device:TPU:1, one launch (start us, length us, event | category | flops | bytes accessed | tf_op | source)
XLA Modules:
  0.0 80.1 jit_solution(15199629123182746049)
XLA Ops:
  0.6 77.2 %distill_step.1 = (f32[32,128]{1,0:T(8,128)}, bf16[192,384]{1,0:T(8,128)(2,1)}) custom-call(bf16[8,4,64]{2,1,0:T(4,128)(2,1)} %args_0_.4, bf16[8,4,64]{2,1,0:T(4,128)(2,1)} %args_1_.4, s32[8]{0:T(128)} %args_2_.4, bf16[1,64,3072]{2,1,0:T(8,128)(2,1)} %args_3_.4, f32[1,3072]{1,0:T(1,128)} %args_4_.4, bf16[1,16,24,384]{3,2,1,0:T(8,128)(2,1)} %args_5_.4, ...), custom_call_target="tpu_custom_call" | custom-call | tf_op jit(solution)/shard_map/distill_step/pallas_call | solution.py:666
  77.8 0.0 copy-start
  77.8 1.6 %convert_bitcast_fusion = f32[16,12,384]{2,0,1:T(8,128)} fusion(bf16[12,16,384]{2,1,0:T(8,128)(2,1)} %bitcast.8), kind=kLoop, calls=%fused_computation | loop fusion | flops 73728 | bytes 442368 | tf_op jit(solution)/shard_map/transpose | solution.py:681
  79.5 0.0 copy-done
  79.5 0.6 copy.12
Async XLA Ops:
  77.8 1.7 %copy-start = (f32[32,128]{1,0:T(8,128)S(1)}, f32[32,128]{1,0:T(8,128)}, u32[]{:S(2)}) copy-start(f32[32,128]{1,0:T(8,128)} %get-tuple-element.4) | copy-start | bytes 49156
